TPU v7x, 256 devices: a whole 4x4x8 slice. The times are simulated.
256 devices in a mesh: gx: 4 (over x), gy: 8 (over z), gz: 8 (over y, core).
Axes of the slice: x: 4, y: 4, z: 8, core: 2. Of those that a mesh axis runs over, the one named last changes fastest.
Arguments:
- rhs: float32 [64, 128, 1024], P('gx', 'gy', 'gz'), may hold values from -6 to 6
- face_x: float32 [64, 128, 1024], P('gx', 'gy', 'gz'), may hold values from 0.25 to 4
- face_y: float32 [64, 128, 1024], P('gx', 'gy', 'gz'), may hold values from 0.25 to 4
- face_z: float32 [64, 128, 1024], P('gx', 'gy', 'gz'), may hold values from 0.25 to 4
Outputs:
- solution: float32 [64, 128, 1024], P('gx', 'gy', 'gz')
All inputs are finite; a program needn't handle non-finite values.
Results may differ from a plain program's by a relative error of at most 0.00002.
Values sent between devices are 32-bit elements; how exact they have to be, the bound alone decides.
A program may use at most 64 MiB of HBM per device.

v0:
```python
import jax
import jax.numpy as jnp
from jax import lax
from jax.experimental import pallas as pl
from jax.experimental.pallas import tpu as pltpu
from jax.sharding import PartitionSpec as P

RELAX = 2.0 / 3.0
THIRD = 1.0 / 3.0
COARSE_SWEEPS = 24
GX, GY, GZ = 4, 8, 8
F32 = jnp.float32
MESH = pl.DeviceIdType.MESH

FACES = [(1, 0, 0), (-1, 0, 0), (0, 1, 0), (0, -1, 0), (0, 0, 1), (0, 0, -1)]
DOWN = [(-1, 0, 0), (0, -1, 0), (0, 0, -1)]
RING_Z = [(0, 0, k) for k in (4, 3, 5, 2, 6, 1, 7)]
RING_Y = [(0, k, 0) for k in (4, 3, 5, 2, 6, 1, 7)]
PLANE = [(2, 1, 0), (2, -1, 0), (1, 1, 0), (1, -1, 0), (3, 1, 0), (3, -1, 0)]
PLANE += [(2, 0, 0), (0, 1, 0), (0, -1, 0), (1, 0, 0), (3, 0, 0)]


def lanes(rows):
    return lax.broadcasted_iota(jnp.int32, (rows, 128), 1)


def sublanes(rows):
    return lax.broadcasted_iota(jnp.int32, (rows, 128), 0)


def turn(value, steps, axis=1):
    steps %= value.shape[axis]
    return value if steps == 0 else pltpu.roll(value, steps, axis)


def take(value, index):
    return jnp.take_along_axis(value, index, axis=1, mode="promise_in_bounds")


class Block:
    def __init__(self, size_x, size_y, size_z, weight):
        self.X, self.Y, self.Z, self.weight = size_x, size_y, size_z, weight
        self.pitch = size_y + 8
        self.rows = size_x * size_y
        self.padded = 8 + (size_x + 2) * self.pitch

    def base(self, i):
        return 8 + (i + 1) * self.pitch

    def own(self, i):
        return pl.ds(i * self.Y, self.Y)

    def at(self, i, shift=0):
        return pl.ds(self.base(i) + shift, self.Y)

    def row_of_each(self, y):
        return pl.ds(self.base(0) + y, self.X, stride=self.pitch)


B0 = Block(16, 16, 128, 1.0)
B1 = Block(8, 8, 64, 0.25)
BLOCKS = (B0, B1)

SCRATCH = {}


def vmem(name, *shape):
    SCRATCH[name] = pltpu.VMEM(shape, F32)


def dma(name, *shape):
    SCRATCH[name] = pltpu.SemaphoreType.DMA(shape)


for key in ("rhs", "fx", "fy", "fz"):
    vmem(key, 256, 128)
dma("in_sem", 5)
for level, block in enumerate(BLOCKS):
    for key in ("cxl", "cxu", "cyl", "cyu", "czl", "czu", "g", "d15", "kw", "r", "w"):
        vmem(f"{key}{level}", block.rows, 128)
    vmem(f"va{level}", block.padded, 128)
    vmem(f"vb{level}", block.padded, 128)
    vmem(f"lyp{level}", block.X * block.pitch, 128)
for key in ("fx1", "fy1", "fz1"):
    vmem(key, 64, 128)
for key, rows, count in (
    ("a0", 16, 3), ("a1", 8, 3), ("b", 16, 6), ("c", 16, 6), ("d", 8, 6),
    ("e", 8, 6), ("f", 8, 6), ("q", 8, 6), ("h", 16, 6),
):
    vmem(f"{key}_snd", count, rows, 128)
    vmem(f"{key}_rcv", count, rows, 128)
    dma(f"{key}_ss", count)
    dma(f"{key}_rs", count)
vmem("t16", 3, 16, 128)
for key, arrays in (("zf", 3), ("zr", 1)):
    vmem(f"{key}_snd", 16, 128)
    vmem(f"{key}_rcv", 7, 16, 128)
    dma(f"{key}_ss", 7)
    dma(f"{key}_rs", 7)
for key, arrays in (("xf", 3), ("xr", 1)):
    vmem(f"{key}_snd", arrays * 2, 16, 128)
    vmem(f"{key}_rcv", 11, arrays * 2, 16, 128)
    dma(f"{key}_ss", 11)
    dma(f"{key}_rs", 11)
for key in ("f2", "lx2", "ly2", "lz2", "va2", "vb2"):
    vmem(key, 36, 16, 128)
for key in ("cxl2", "cxu2", "cyl2", "cyu2", "czl2", "czu2", "g2", "d152", "kw2"):
    vmem(key, 36, 16, 128)
vmem("s2", 128, 128)
vmem("p2", 256, 128)
vmem("face3", 3, 128, 128)
vmem("f3", 128, 128)
for key in ("yf", "yr"):
    dma(f"{key}_ss", 7)
    dma(f"{key}_rs", 7)
for key in ("cxl3", "cxu3", "cyl3", "cyu3", "czl3", "czu3", "g3", "d153", "kw3", "r3", "p3"):
    vmem(key, 128, 128)
vmem("va3", 160, 128)
vmem("vb3", 160, 128)
for key in ("t4", "cxl4", "cxu4", "cyl4", "cyu4", "czl4", "czu4", "d154", "kw4", "r4", "p4"):
    vmem(key, 32, 128)
vmem("fc4", 3, 32, 128)
for key in ("t5", "cx5", "cyl5", "cyu5", "czl5", "czu5", "kw5", "e5"):
    vmem(key, 8, 128)
vmem("q1", 96, 128)
vmem("h1", 6, 8, 128)


class Space:
    pass


def cycle(rhs_in, fx_in, fy_in, fz_in, out, *scratch):
    s = Space()
    for name, ref in zip(SCRATCH, scratch):
        setattr(s, name, ref)
    gx, gy, gz = lax.axis_index("gx"), lax.axis_index("gy"), lax.axis_index("gz")

    def peer(offset):
        return (
            (gx + offset[0]) & (GX - 1),
            (gy + offset[1]) & (GY - 1),
            (gz + offset[2]) & (GZ - 1),
        )

    loads = [
        pltpu.make_async_copy(source, target, s.in_sem.at[k])
        for k, (source, target) in enumerate(
            ((fx_in, s.fx), (fy_in, s.fy), (fz_in, s.fz), (rhs_in, s.rhs))
        )
    ]
    for load in loads:
        load.start()

    barrier = pltpu.get_barrier_semaphore()
    friends = list(dict.fromkeys(RING_Y + RING_Z + PLANE))
    friends = list(dict.fromkeys((x & 3, y & 7, z & 7) for x, y, z in friends))
    for offset in friends:
        pl.semaphore_signal(barrier, inc=1, device_id=peer(offset), device_id_type=MESH)

    def copies(offsets, sources, targets, ss, rs):
        made = [
            pltpu.make_async_remote_copy(
                src_ref=sources(k),
                dst_ref=targets(k),
                send_sem=ss.at[k],
                recv_sem=rs.at[k],
                device_id=peer(offset),
                device_id_type=MESH,
            )
            for k, offset in enumerate(offsets)
        ]
        for one in made:
            one.start()
        return made

    def finish(made):
        for one in made:
            one.wait_recv()
        for one in made:
            one.wait_send()

    def flag(condition):
        return jnp.where(condition, 1.0, 0.0).astype(F32)

    low_x, low_y, low_z = flag(gx > 0), flag(gy > 0), flag(gz > 0)
    top_x, top_y, top_z = flag(gx < GX - 1), flag(gy < GY - 1), flag(gz < GZ - 1)


    def pack(read, block, column):
        packed = jnp.zeros((block.Y, 128), F32)
        lane = lanes(block.Y)
        for i in range(block.X):
            packed = jnp.where(lane == i, turn(read(i), i - column), packed)
        return packed

    def send_faces(block, ref, key):
        snd = getattr(s, key + "_snd")
        snd[0] = ref[block.at(block.X - 1)]
        snd[1] = ref[block.at(0)]
        snd[2] = ref[block.row_of_each(block.Y - 1)]
        snd[3] = ref[block.row_of_each(0)]
        snd[4] = pack(lambda i: ref[block.at(i)], block, block.Z - 1)
        snd[5] = pack(lambda i: ref[block.at(i)], block, 0)
        rcv = getattr(s, key + "_rcv")
        return copies(
            FACES,
            lambda k: snd.at[k],
            lambda k: rcv.at[k],
            getattr(s, key + "_ss"),
            getattr(s, key + "_rs"),
        )

    def fill(block, ref, halo):
        ref[block.at(-1)] = halo[0]
        ref[block.at(block.X)] = halo[1]
        ref[block.row_of_each(-1)] = halo[2]
        ref[block.row_of_each(block.Y)] = halo[3]

    def send_upper(level, lx, ly, lz, key):
        block = BLOCKS[level]
        snd = getattr(s, key + "_snd")
        snd[0] = lx[block.own(0)]
        snd[1] = ly[pl.ds(0, block.X, stride=block.Y)]
        snd[2] = pack(lambda i: lz[block.own(i)], block, 0)
        rcv = getattr(s, key + "_rcv")
        return copies(
            DOWN,
            lambda k: snd.at[k],
            lambda k: rcv.at[k],
            getattr(s, key + "_ss"),
            getattr(s, key + "_rs"),
        )

    def coefficients(level, lx, ly, lz, key):
        block = BLOCKS[level]
        rcv = getattr(s, key + "_rcv")
        lyp = getattr(s, f"lyp{level}")
        c = {k: getattr(s, f"{k}{level}") for k in ("cxl", "cxu", "cyl", "cyu", "czl", "czu")}
        d15, kw = getattr(s, f"d15{level}"), getattr(s, f"kw{level}")
        for i in range(block.X):
            lyp[pl.ds(i * block.pitch, block.Y)] = ly[block.own(i)]
        lyp[pl.ds(block.Y, block.X, stride=block.pitch)] = rcv[1] * top_y
        next_x = rcv[0] * top_x
        next_z = rcv[2] * top_z
        lane, row = lanes(block.Y), sublanes(block.Y)
        keep_y = jnp.where(row == 0, low_y, 1.0)
        keep_z = jnp.where(lane == 0, low_z, 1.0)
        for i in range(block.X):
            own = block.own(i)
            a_xl = lx[own]
            a_xu = lx[block.own(i + 1)] if i + 1 < block.X else next_x
            a_yl = ly[own]
            a_yu = lyp[pl.ds(i * block.pitch + 1, block.Y)]
            a_zl = lz[own]
            a_zu = jnp.where(
                lane == block.Z - 1, turn(next_z, block.Z - 1 - i), turn(a_zl, -1)
            )
            total = (a_xl + a_yl + a_zl) + (a_xu + a_yu + a_zu)
            scale = RELAX / total
            d15[own] = (1.5 * block.weight) * total
            kw[own] = scale * (1.0 / block.weight)
            c["cxl"][own] = scale * a_xl * (low_x if i == 0 else 1.0)
            c["cxu"][own] = scale * a_xu
            c["cyl"][own] = scale * a_yl * keep_y
            c["cyu"][own] = scale * a_yu
            c["czl"][own] = scale * a_zl * keep_z
            c["czu"][own] = scale * a_zu

    def stencil(level, ref, low, high, emit):
        block = BLOCKS[level]
        lane = lanes(block.Y)
        get = lambda k: getattr(s, f"{k}{level}")
        for i in range(block.X):
            own = block.own(i)
            v = ref[block.at(i)]
            down = jnp.where(lane == 0, turn(low, -i), turn(v, 1))
            up = jnp.where(lane == block.Z - 1, turn(high, block.Z - 1 - i), turn(v, -1))
            t_x = get("cxl")[own] * ref[block.at(i - 1)] + get("cxu")[own] * ref[block.at(i + 1)]
            t_y = get("cyl")[own] * ref[block.at(i, -1)] + get("cyu")[own] * ref[block.at(i, 1)]
            t_z = get("czl")[own] * down + get("czu")[own] * up
            emit(i, v, get("g")[own] + (t_x + t_y + t_z))

    def smooth(level, source, target, low, high):
        block = BLOCKS[level]

        def emit(i, v, total):
            target[block.at(i)] = v * THIRD + total

        stencil(level, source, low, high, emit)

    def residual(level, source, low, high):
        block = BLOCKS[level]
        d15, r = getattr(s, f"d15{level}"), getattr(s, f"r{level}")

        def emit(i, v, total):
            r[block.own(i)] = d15[block.own(i)] * (total - RELAX * v)

        stencil(level, source, low, high, emit)

    lane8, lane16 = lanes(8), lanes(16)
    even8 = (2 * lane8) & 127
    half16 = lane16 >> 1

    def pair_z(value):
        return value + turn(value, -1)

    def stage_z(arrays, snd):
        group = lane16 >> 4
        packed = jnp.zeros((16, 128), F32)
        for a in range(arrays):
            whole = s.t16[a]
            for p in range(2):
                moved = take(whole, 4 * (lane16 & 15) + 2 * p)
                packed = jnp.where(group == ((gz + 2 * a + p) & 7), moved, packed)
        snd[...] = packed

    def merge_z(arrays, snd, rcv, target):
        group = lane16 >> 4
        parts = [(0, snd[...])] + [(RING_Z[k][2], rcv[k]) for k in range(7)]
        for q in range(2 * arrays):
            merged = jnp.zeros((16, 128), F32)
            for distance, part in parts:
                merged = jnp.where(group == ((gz - distance + q) & 7), part, merged)
            target[q] = turn(merged, -16 * q)

    for load in loads[:3]:
        load.wait()
    for i in range(8):
        own = pl.ds(8 * i, 8)
        here = lambda ref, shift: ref[pl.ds(32 * i + shift, 8, stride=2)]
        s.fx1[own] = take(pair_z(here(s.fx, 0) + here(s.fx, 1)), even8) * 0.25
        s.fy1[own] = take(pair_z(here(s.fy, 0) + here(s.fy, 16)), even8) * 0.25
        total = (here(s.fz, 0) + here(s.fz, 1)) + (here(s.fz, 16) + here(s.fz, 17))
        s.fz1[own] = take(total, even8) * 0.25
    for i in range(4):
        own = pl.ds(4 * i, 4)
        here = lambda ref, shift: ref[pl.ds(16 * i + shift, 4, stride=2)]
        s.t16[0, own] = here(s.fx1, 0) + here(s.fx1, 1)
        s.t16[1, own] = here(s.fy1, 0) + here(s.fy1, 8)
        total = (here(s.fz1, 0) + here(s.fz1, 1)) + (here(s.fz1, 8) + here(s.fz1, 9))
        s.t16[2, own] = total * 0.25
    s.t16[0] = pair_z(s.t16[0]) * 0.25
    s.t16[1] = pair_z(s.t16[1]) * 0.25
    stage_z(3, s.zf_snd)
    for ref in (s.va0, s.vb0, s.va1, s.vb1):
        ref[...] = jnp.zeros_like(ref)
    for ref in (s.lx2, s.ly2, s.lz2):
        ref[...] = jnp.ones_like(ref)
    for ref in (s.f2, s.va2, s.vb2):
        ref[...] = jnp.zeros_like(ref)
    for ref in (s.va3, s.vb3, s.p2):
        ref[...] = jnp.zeros_like(ref)

    pl.semaphore_wait(barrier, len(friends))
    round_a0 = send_upper(0, s.fx, s.fy, s.fz, "a0")
    round_a1 = send_upper(1, s.fx1, s.fy1, s.fz1, "a1")
    round_zf = copies(
        RING_Z, lambda k: s.zf_snd, lambda k: s.zf_rcv.at[k], s.zf_ss, s.zf_rs
    )
    loads[3].wait()
    finish(round_a0)
    coefficients(0, s.fx, s.fy, s.fz, "a0")
    for i in range(16):
        own = B0.own(i)
        start = s.kw0[own] * s.rhs[own]
        s.g0[own] = start
        s.va0[B0.at(i)] = start
    round_b = send_faces(B0, s.va0, "b")
    finish(round_a1)
    coefficients(1, s.fx1, s.fy1, s.fz1, "a1")
    finish(round_b)
    fill(B0, s.va0, s.b_rcv)
    smooth(0, s.va0, s.vb0, s.b_rcv[4], s.b_rcv[5])
    round_c = send_faces(B0, s.vb0, "c")
    finish(round_zf)
    merge_z(3, s.zf_snd, s.zf_rcv, s.xf_snd)
    finish(round_c)
    round_xf = copies(
        PLANE, lambda k: s.xf_snd, lambda k: s.xf_rcv.at[k], s.xf_ss, s.xf_rs
    )
    fill(B0, s.vb0, s.c_rcv)
    residual(0, s.vb0, s.c_rcv[4], s.c_rcv[5])

    for i in range(8):
        own = pl.ds(8 * i, 8)
        here = lambda shift: s.r0[pl.ds(32 * i + shift, 8, stride=2)]
        total = (here(0) + here(1)) + (here(16) + here(17))
        start = s.kw1[own] * (take(pair_z(total), even8) * 0.125)
        s.g1[own] = start
        s.va1[B1.at(i)] = start
    round_d = send_faces(B1, s.va1, "d")
    finish(round_d)
    fill(B1, s.va1, s.d_rcv)
    smooth(1, s.va1, s.vb1, s.d_rcv[4], s.d_rcv[5])
    round_e = send_faces(B1, s.vb1, "e")


    def block2(p, x):
        return 18 * p + 1 + x

    def spread(arrays, snd, rcv, targets):
        parts = [((0, 0, 0), lambda q: snd.at[q])]
        for k in range(11):
            parts.append((PLANE[k], lambda q, k=k: rcv.at[k, q]))
        for offset, part in parts:
            first = 4 * ((gx - offset[0]) & 3)
            place = pl.ds(4 * (1 - offset[1]), 4)
            for a in range(arrays):
                for p in range(2):
                    for x in range(4):
                        piece = part(2 * a + p)[pl.ds(4 * x, 4)]
                        targets[a][block2(p, x) + first, place] = piece

    finish(round_xf)
    spread(3, s.xf_snd, s.xf_rcv, (s.lx2, s.ly2, s.lz2))
    row16 = sublanes(16)
    global_y = row16 + 4 * gy - 4
    not_low, not_top = global_y != 0, global_y != 4 * GY - 1

    for a, ref in enumerate((s.lx2, s.ly2, s.lz2)):
        for i in range(8):
            total = ref[block2(0, 2 * i)]
            if a != 2:
                total = total + ref[block2(1, 2 * i)]
            if a != 0:
                total = total + ref[block2(0, 2 * i + 1)]
            if a == 1:
                total = total + ref[block2(1, 2 * i + 1)]
            s.s2[pl.ds(16 * i, 16)] = total
        for j in range(2):
            total = s.s2[pl.ds(4 + 2 * j, 8, stride=16)]
            if a != 1:
                total = total + s.s2[pl.ds(5 + 2 * j, 8, stride=16)]
            s.face3[a, pl.ds(pl.multiple_of(16 * gy + 8 * j, 8), 8)] = total * 0.25
    mine = pl.ds(pl.multiple_of(16 * gy, 16), 16)
    round_yf = copies(
        RING_Y,
        lambda k: s.face3.at[:, mine],
        lambda k: s.face3.at[:, mine],
        s.yf_ss,
        s.yf_rs,
    )

    for p in range(2):
        for x in range(16):
            j = block2(p, x)
            a_xl, a_yl, a_zl = s.lx2[j], s.ly2[j], s.lz2[j]
            a_xu = s.lx2[j + 1] if x < 15 else jnp.zeros((16, 128), F32)
            a_yu = jnp.where(not_top, turn(a_yl, -1, 0), 0.0)
            if p == 0:
                a_zu = s.lz2[block2(1, x)]
            else:
                a_zu = jnp.where(lane16 == 127, 0.0, turn(s.lz2[block2(0, x)], -1))
            total = (a_xl + a_yl + a_zl) + (a_xu + a_yu + a_zu)
            scale = RELAX / total
            s.d152[j] = (1.5 * 0.0625) * total
            s.kw2[j] = scale * 16.0
            s.cxl2[j] = scale * a_xl if x > 0 else jnp.zeros((16, 128), F32)
            s.cxu2[j] = scale * a_xu
            s.cyl2[j] = jnp.where(not_low, scale * a_yl, 0.0)
            s.cyu2[j] = scale * a_yu
            s.czl2[j] = scale * a_zl if p == 1 else jnp.where(lane16 == 0, 0.0, scale * a_zl)
            s.czu2[j] = scale * a_zu

    def stencil2(ref, emit):
        for p in range(2):
            for x in range(16):
                j, other = block2(p, x), block2(1 - p, x)
                v, w = ref[j], ref[other]
                t_x = s.cxl2[j] * ref[j - 1] + s.cxu2[j] * ref[j + 1]
                t_y = s.cyl2[j] * turn(v, 1, 0) + s.cyu2[j] * turn(v, -1, 0)
                down, up = (turn(w, 1), w) if p == 0 else (w, turn(w, -1))
                t_z = s.czl2[j] * down + s.czu2[j] * up
                emit(j, v, s.g2[j] + (t_x + t_y + t_z))

    def smooth2(source, target):
        def emit(j, v, total):
            target[j] = v * THIRD + total

        stencil2(source, emit)

    finish(round_e)
    fill(B1, s.vb1, s.e_rcv)
    residual(1, s.vb1, s.e_rcv[4], s.e_rcv[5])
    for i in range(4):
        here = lambda shift: s.r1[pl.ds(16 * i + shift, 4, stride=2)]
        s.t16[0, pl.ds(4 * i, 4)] = (here(0) + here(1)) + (here(8) + here(9))
    s.t16[0] = pair_z(s.t16[0]) * 0.125
    stage_z(1, s.zr_snd)
    round_zr = copies(
        RING_Z, lambda k: s.zr_snd, lambda k: s.zr_rcv.at[k], s.zr_ss, s.zr_rs
    )

    finish(round_yf)
    row8 = sublanes(8)
    zero8 = jnp.zeros((8, 128), F32)
    for y in range(16):
        own = pl.ds(8 * y, 8)
        a_xl, a_yl, a_zl = s.face3[0, own], s.face3[1, own], s.face3[2, own]
        a_xu = jnp.where(row8 == 7, 0.0, turn(a_xl, -1, 0))
        a_yu = s.face3[1, pl.ds(8 * y + 8, 8)] if y < 15 else zero8
        a_zu = jnp.where(lane8 == 127, 0.0, turn(a_zl, -1))
        total = (a_xl + a_yl + a_zl) + (a_xu + a_yu + a_zu)
        scale = RELAX / total
        s.d153[own] = (1.5 * 0.25**3) * total
        s.kw3[own] = scale * 64.0
        s.cxl3[own] = jnp.where(row8 == 0, 0.0, scale * a_xl)
        s.cxu3[own] = scale * a_xu
        s.cyl3[own] = scale * a_yl if y > 0 else zero8
        s.cyu3[own] = scale * a_yu
        s.czl3[own] = jnp.where(lane8 == 0, 0.0, scale * a_zl)
        s.czu3[own] = scale * a_zu

    lane32, row32 = lanes(32), sublanes(32)

    def both(value, lane, step):
        return value + jnp.where(
            (lane & step) == 0, turn(value, -step), turn(value, step)
        )

    def lower_of(value, lane, step):
        return jnp.where((lane & step) == 0, value, turn(value, step))

    for a in range(3):
        for y in range(8):
            here = lambda shift: s.face3[a, pl.ds(16 * y + shift, 4, stride=2)]
            if a == 0:
                total = here(0) + here(8)
            elif a == 1:
                total = here(0) + here(1)
            else:
                total = (here(0) + here(1)) + (here(8) + here(9))
            s.t4[pl.ds(4 * y, 4)] = total
        total = s.t4[...]
        total = both(total, lane32, 1) if a < 2 else lower_of(total, lane32, 1)
        s.fc4[a] = total * 0.25
    a_xl, a_yl, a_zl = s.fc4[0], s.fc4[1], s.fc4[2]
    a_xu = jnp.where((row32 & 3) == 3, 0.0, turn(a_xl, -1, 0))
    a_yu = jnp.where(row32 >= 28, 0.0, turn(a_yl, -4, 0))
    a_zu = jnp.where(lane32 >= 126, 0.0, turn(a_zl, -2))
    total = (a_xl + a_yl + a_zl) + (a_xu + a_yu + a_zu)
    scale = RELAX / total
    s.d154[...] = (1.5 * 0.25**4) * total
    s.kw4[...] = scale * 256.0
    s.cxl4[...] = jnp.where((row32 & 3) == 0, 0.0, scale * a_xl)
    s.cxu4[...] = scale * a_xu
    s.cyl4[...] = jnp.where(row32 < 4, 0.0, scale * a_yl)
    s.cyu4[...] = scale * a_yu
    s.czl4[...] = jnp.where(lane32 < 2, 0.0, scale * a_zl)
    s.czu4[...] = scale * a_zu

    faces5 = []
    for a in range(3):
        for x in range(2):
            here = lambda shift: s.fc4[a, pl.ds(2 * x + shift, 4, stride=8)]
            if a == 0:
                total = here(0) + here(4)
            elif a == 1:
                total = here(0) + here(1)
            else:
                total = (here(0) + here(1)) + (here(4) + here(5))
            s.t5[pl.ds(4 * x, 4)] = total
        total = s.t5[...]
        total = both(total, lane8, 2) if a < 2 else lower_of(total, lane8, 2)
        faces5.append(total * 0.25)
    a_xl, a_yl, a_zl = faces5
    a_xu = jnp.where(row8 >= 4, 0.0, turn(a_xl, 4, 0))
    a_yu = jnp.where((row8 & 3) == 3, 0.0, turn(a_yl, -1, 0))
    a_zu = jnp.where(lane8 >= 124, 0.0, turn(a_zl, -4))
    total = (a_xl + a_yl + a_zl) + (a_xu + a_yu + a_zu)
    scale = RELAX / total
    s.kw5[...] = scale * 1024.0
    s.cx5[...] = jnp.where(row8 >= 4, scale * a_xl, scale * a_xu)
    s.cyl5[...] = jnp.where((row8 & 3) == 0, 0.0, scale * a_yl)
    s.cyu5[...] = scale * a_yu
    s.czl5[...] = jnp.where(lane8 < 4, 0.0, scale * a_zl)
    s.czu5[...] = scale * a_zu

    finish(round_zr)
    merge_z(1, s.zr_snd, s.zr_rcv, s.xr_snd)
    round_xr = copies(
        PLANE, lambda k: s.xr_snd, lambda k: s.xr_rcv.at[k], s.xr_ss, s.xr_rs
    )
    finish(round_xr)
    spread(1, s.xr_snd, s.xr_rcv, (s.f2,))
    for p in range(2):
        for x in range(16):
            j = block2(p, x)
            start = s.kw2[j] * s.f2[j]
            s.g2[j] = start
            s.va2[j] = start
    smooth2(s.va2, s.vb2)

    def emit_r2(j, v, total):
        s.f2[j] = s.d152[j] * (total - RELAX * v)

    stencil2(s.vb2, emit_r2)
    for i in range(8):
        total = (s.f2[block2(0, 2 * i)] + s.f2[block2(1, 2 * i)]) + (
            s.f2[block2(0, 2 * i + 1)] + s.f2[block2(1, 2 * i + 1)]
        )
        s.s2[pl.ds(16 * i, 16)] = total
    for j in range(2):
        total = s.s2[pl.ds(4 + 2 * j, 8, stride=16)] + s.s2[pl.ds(5 + 2 * j, 8, stride=16)]
        s.f3[pl.ds(pl.multiple_of(16 * gy + 8 * j, 8), 8)] = total * 0.125
    round_yr = copies(
        RING_Y, lambda k: s.f3.at[mine], lambda k: s.f3.at[mine], s.yr_ss, s.yr_rs
    )
    finish(round_yr)

    def at3(y):
        return pl.ds(16 + 8 * y, 8)

    def stencil3(ref, emit):
        for y in range(16):
            own = pl.ds(8 * y, 8)
            v = ref[at3(y)]
            t_x = s.cxl3[own] * turn(v, 1, 0) + s.cxu3[own] * turn(v, -1, 0)
            t_y = s.cyl3[own] * ref[at3(y - 1)] + s.cyu3[own] * ref[at3(y + 1)]
            t_z = s.czl3[own] * turn(v, 1) + s.czu3[own] * turn(v, -1)
            emit(y, v, s.g3[own] + (t_x + t_y + t_z))

    def smooth3(source, target):
        def emit(y, v, total):
            target[at3(y)] = v * THIRD + total

        stencil3(source, emit)

    for y in range(16):
        own = pl.ds(8 * y, 8)
        start = s.kw3[own] * s.f3[own]
        s.g3[own] = start
        s.va3[at3(y)] = start
    smooth3(s.va3, s.vb3)

    def emit_r3(y, v, total):
        own = pl.ds(8 * y, 8)
        s.r3[own] = s.d153[own] * (total - RELAX * v)

    stencil3(s.vb3, emit_r3)
    for y in range(8):
        here = lambda shift: s.r3[pl.ds(16 * y + shift, 4, stride=2)]
        s.t4[pl.ds(4 * y, 4)] = (here(0) + here(1)) + (here(8) + here(9))
    f4 = both(s.t4[...], lane32, 1) * 0.125

    def total4(v):
        t_x = s.cxl4[...] * turn(v, 1, 0) + s.cxu4[...] * turn(v, -1, 0)
        t_y = s.cyl4[...] * turn(v, 4, 0) + s.cyu4[...] * turn(v, -4, 0)
        t_z = s.czl4[...] * turn(v, 2) + s.czu4[...] * turn(v, -2)
        return g4 + (t_x + t_y + t_z)

    g4 = s.kw4[...] * f4
    v4 = g4
    v4 = v4 * THIRD + total4(v4)
    s.r4[...] = s.d154[...] * (total4(v4) - RELAX * v4)
    for x in range(2):
        here = lambda shift: s.r4[pl.ds(2 * x + shift, 4, stride=8)]
        s.t5[pl.ds(4 * x, 4)] = (here(0) + here(1)) + (here(4) + here(5))
    g5 = s.kw5[...] * (both(s.t5[...], lane8, 2) * 0.125)
    cx5, cyl5, cyu5, czl5, czu5 = s.cx5[...], s.cyl5[...], s.cyu5[...], s.czl5[...], s.czu5[...]

    def sweep5(index, v):
        t_y = cyl5 * turn(v, 1, 0) + cyu5 * turn(v, -1, 0)
        t_z = czl5 * turn(v, 4) + czu5 * turn(v, -4)
        return (v * THIRD + g5) + (cx5 * turn(v, 4, 0) + (t_y + t_z))

    s.e5[...] = lax.fori_loop(0, COARSE_SWEEPS - 1, sweep5, g5)
    for x in range(2):
        piece = s.e5[pl.ds(4 * x, 4)]
        for shift in (0, 1, 4, 5):
            s.p4[pl.ds(2 * x + shift, 4, stride=8)] = piece
    v4 = v4 + s.p4[...]
    v4 = v4 * THIRD + total4(v4)
    v4 = v4 * THIRD + total4(v4)
    s.r4[...] = v4
    for x in range(4):
        piece = s.r4[pl.ds(x, 8, stride=4)]
        for shift in (0, 1, 8, 9):
            s.p3[pl.ds(2 * x + shift, 8, stride=16)] = piece
    for y in range(16):
        s.vb3[at3(y)] = s.vb3[at3(y)] + s.p3[pl.ds(8 * y, 8)]
    smooth3(s.vb3, s.va3)
    smooth3(s.va3, s.vb3)

    for k in range(6):
        piece = s.vb3[pl.ds(pl.multiple_of(16 * gy + 8 * k, 8), 8)]
        for x in range(2):
            for y in range(2):
                s.p2[pl.ds(16 * x + 2 * k + y, 8, stride=32)] = piece
    for x in range(16):
        more = s.p2[pl.ds(16 * x, 16)]
        for p in range(2):
            s.vb2[block2(p, x)] = s.vb2[block2(p, x)] + more
    smooth2(s.vb2, s.va2)
    smooth2(s.va2, s.vb2)

    signed = jnp.where(lane16 < 96, lane16, lane16 - 128)
    index = (16 * gz + (signed >> 2)) & 127
    odd = ((signed >> 1) & 1) == 1
    for k in range(6):
        x = 4 * gx + k - 1
        s.q1[pl.ds(16 * k, 16)] = jnp.where(
            odd, take(s.vb2[block2(1, x)], index), take(s.vb2[block2(0, x)], index)
        )
    for k, source in ((0, 0), (1, 5)):
        for y in range(2):
            s.h1[k, pl.ds(y, 4, stride=2)] = s.q1[pl.ds(16 * source + 4, 4)]
    for k, source in ((2, 3), (3, 8)):
        for x in range(2):
            s.h1[k, pl.ds(x, 4, stride=2)] = s.q1[pl.ds(16 + source, 4, stride=16)]
    for i in range(8):
        for y in range(2):
            s.w1[pl.ds(8 * i + y, 4, stride=2)] = s.q1[pl.ds(16 * (i // 2 + 1) + 4, 4)]
    s.h1[4] = pack(lambda i: s.w1[B1.own(i)], B1, 127)
    s.h1[5] = pack(lambda i: s.w1[B1.own(i)], B1, 64)
    for k in range(6):
        s.h1[k] = s.h1[k] + s.e_rcv[k]
    for i in range(8):
        s.vb1[B1.at(i)] = s.vb1[B1.at(i)] + s.w1[B1.own(i)]
    fill(B1, s.vb1, s.h1)
    smooth(1, s.vb1, s.va1, s.h1[4], s.h1[5])
    round_f = send_faces(B1, s.va1, "f")
    finish(round_f)
    fill(B1, s.va1, s.f_rcv)
    smooth(1, s.va1, s.vb1, s.f_rcv[4], s.f_rcv[5])
    round_q = send_faces(B1, s.vb1, "q")

    def widen(value, ref, start):
        ref[pl.ds(start, 8, stride=2)] = value
        ref[pl.ds(start + 1, 8, stride=2)] = value
        return take(ref[pl.ds(start, 16)], half16)

    for i in range(8):
        more = widen(s.vb1[B1.at(i)], s.w0, 16 * i)
        for x in (2 * i, 2 * i + 1):
            s.vb0[B0.at(x)] = s.vb0[B0.at(x)] + more
    finish(round_q)
    for k in range(6):
        s.c_rcv[k] = s.c_rcv[k] + widen(s.q_rcv[k], s.w0, 128 + 16 * k)
    fill(B0, s.vb0, s.c_rcv)
    smooth(0, s.vb0, s.va0, s.c_rcv[4], s.c_rcv[5])
    round_h = send_faces(B0, s.va0, "h")
    finish(round_h)
    fill(B0, s.va0, s.h_rcv)

    def emit_out(i, v, total):
        out[B0.own(i)] = v * THIRD + total

    stencil(0, s.va0, s.h_rcv[4], s.h_rcv[5], emit_out)


def shards(rhs, face_x, face_y, face_z):
    flat = [a.reshape(256, 128) for a in (rhs, face_x, face_y, face_z)]
    whole = pl.pallas_call(
        cycle,
        out_shape=jax.ShapeDtypeStruct((256, 128), F32),
        in_specs=[pl.BlockSpec(memory_space=pl.ANY)] * 4,
        out_specs=pl.BlockSpec(memory_space=pltpu.VMEM),
        scratch_shapes=list(SCRATCH.values()),
        compiler_params=pltpu.CompilerParams(
            collective_id=0, has_side_effects=True, vmem_limit_bytes=48 * 1024 * 1024
        ),
        name="vcycle",
    )(*flat)
    return whole.reshape(16, 16, 128)


def solution(mesh):
    placed = P("gx", "gy", "gz")
    return jax.shard_map(
        shards, mesh=mesh, in_specs=(placed,) * 4, out_specs=placed, check_vma=False
    )
```

profile of v0, /device:TPU:1, one launch (start us, length us, event | category | flops | bytes accessed | tf_op | source)
XLA Modules:
  0.0 66.2 jit_solution(3356608958400476199)
XLA Ops:
  0.0 0.0 copy-start
  0.0 0.9 %copy-done = f32[16,16,128]{2,1,0:T(8,128)S(1)} copy-done((f32[16,16,128]{2,1,0:T(8,128)S(1)}, f32[16,16,128]{2,1,0:T(8,128)}, u32[]{:S(2)}) %copy-start) | copy-done | bytes 131096
  0.9 0.0 copy-start.1
  0.9 0.9 %copy-done.1 = f32[16,16,128]{2,1,0:T(8,128)S(1)} copy-done((f32[16,16,128]{2,1,0:T(8,128)S(1)}, f32[16,16,128]{2,1,0:T(8,128)}, u32[]{:S(2)}) %copy-start.1) | copy-done | bytes 131096
  1.8 0.0 copy-start.2
  1.8 0.9 %copy-done.2 = f32[16,16,128]{2,1,0:T(8,128)S(1)} copy-done((f32[16,16,128]{2,1,0:T(8,128)S(1)}, f32[16,16,128]{2,1,0:T(8,128)}, u32[]{:S(2)}) %copy-start.2) | copy-done | bytes 131096
  2.7 0.0 copy-start.3
  2.7 0.9 %copy-done.3 = f32[16,16,128]{2,1,0:T(8,128)S(1)} copy-done((f32[16,16,128]{2,1,0:T(8,128)S(1)}, f32[16,16,128]{2,1,0:T(8,128)}, u32[]{:S(2)}) %copy-start.3) | copy-done | bytes 131096
  3.6 62.0 %vcycle.1 = f32[256,128]{1,0:T(8,128)S(1)} custom-call(f32[256,128]{1,0:T(8,128)S(1)} %bitcast.6, f32[256,128]{1,0:T(8,128)S(1)} %bitcast.7, f32[256,128]{1,0:T(8,128)S(1)} %bitcast.8, f32[256,128]{1,0:T(8,128)S(1)} %bitcast.9), custom_call_target="tpu_custom_call" | custom-call | tf_op jit(solution)/shard_map/vcycle/pallas_call | solution.py:755
  65.6 0.7 copy.6
Async XLA Ops:
  0.0 0.9 %copy-start = (f32[16,16,128]{2,1,0:T(8,128)S(1)}, f32[16,16,128]{2,1,0:T(8,128)}, u32[]{:S(2)}) copy-start(f32[16,16,128]{2,1,0:T(8,128)} %param.4) | copy-start | bytes 393220
  0.9 0.9 %copy-start.1 = (f32[16,16,128]{2,1,0:T(8,128)S(1)}, f32[16,16,128]{2,1,0:T(8,128)}, u32[]{:S(2)}) copy-start(f32[16,16,128]{2,1,0:T(8,128)} %param.5) | copy-start | bytes 393220
  1.8 0.9 %copy-start.2 = (f32[16,16,128]{2,1,0:T(8,128)S(1)}, f32[16,16,128]{2,1,0:T(8,128)}, u32[]{:S(2)}) copy-start(f32[16,16,128]{2,1,0:T(8,128)} %param.6) | copy-start | bytes 393220
  2.7 0.9 %copy-start.3 = (f32[16,16,128]{2,1,0:T(8,128)S(1)}, f32[16,16,128]{2,1,0:T(8,128)}, u32[]{:S(2)}) copy-start(f32[16,16,128]{2,1,0:T(8,128)} %param.7) | copy-start | bytes 393220
where the time goes:
time: 66.4 us; the launch traced here: 66.2 us
  Pallas kernels  62 us (93%)
  local copies, waits for them, and re-layouts  4.27 us (6%)
    pallas_call x1, Pallas kernels, shards(): pl.pallas_call(cycle, out_shape=jax.ShapeDtypeStruct((256, 128), F32), in...  62 us
    unnamed x9, local copies, waits for them, and re-layouts  4.27 us

commit v1 on v0

--- a/solution.py
+++ b/solution.py
@@ -16,6 +16,12 @@
 DOWN = [(-1, 0, 0), (0, -1, 0), (0, 0, -1)]
 RING_Z = [(0, 0, k) for k in (4, 3, 5, 2, 6, 1, 7)]
 RING_Y = [(0, k, 0) for k in (4, 3, 5, 2, 6, 1, 7)]
+AROUND = [
+    (x, y, z) for x in (1, -1, 0) for y in (1, -1, 0) for z in (1, -1, 0) if (x, y, z) != (0, 0, 0)
+]
+AROUND.sort(key=lambda d: -(abs(d[0]) + abs(d[1]) + abs(d[2])))
+LINE = [(2, 0, 0), (1, 0, 0), (3, 0, 0)]
+SIDES = [(0, 1, 0), (0, -1, 0)]
 PLANE = [(2, 1, 0), (2, -1, 0), (1, 1, 0), (1, -1, 0), (3, 1, 0), (3, -1, 0)]
 PLANE += [(2, 0, 0), (0, 1, 0), (0, -1, 0), (1, 0, 0), (3, 0, 0)]
 
@@ -58,8 +64,6 @@
 
 
 B0 = Block(16, 16, 128, 1.0)
-B1 = Block(8, 8, 64, 0.25)
-BLOCKS = (B0, B1)
 
 SCRATCH = {}
 
@@ -75,18 +79,36 @@
 for key in ("rhs", "fx", "fy", "fz"):
     vmem(key, 256, 128)
 dma("in_sem", 5)
-for level, block in enumerate(BLOCKS):
-    for key in ("cxl", "cxu", "cyl", "cyu", "czl", "czu", "g", "d15", "kw", "r", "w"):
-        vmem(f"{key}{level}", block.rows, 128)
-    vmem(f"va{level}", block.padded, 128)
-    vmem(f"vb{level}", block.padded, 128)
-    vmem(f"lyp{level}", block.X * block.pitch, 128)
-for key in ("fx1", "fy1", "fz1"):
+for key in ("cxl0", "cxu0", "cyl0", "cyu0", "czl0", "czu0", "g0", "d150", "kw0", "r0", "w0"):
+    vmem(key, 256, 128)
+vmem("va0", B0.padded, 128)
+vmem("vb0", B0.padded, 128)
+vmem("lyp0", B0.X * B0.pitch, 128)
+for key in ("fx1", "fy1", "fz1", "r1"):
     vmem(key, 64, 128)
-for key, rows, count in (
-    ("a0", 16, 3), ("a1", 8, 3), ("b", 16, 6), ("c", 16, 6), ("d", 8, 6),
-    ("e", 8, 6), ("f", 8, 6), ("q", 8, 6), ("h", 16, 6),
-):
+for key in ("cxl1", "cxu1", "cyl1", "cyu1", "czl1", "czu1", "g1", "d151", "kw1"):
+    vmem(key, 17 * 16, 128)
+for key in ("va1", "vb1"):
+    vmem(key, 19 * 16, 128)
+for key, arrays in (("hf", 4), ("hr", 1)):
+    vmem(f"{key}_own", arrays, 8, 8, 128)
+    vmem(f"{key}_low", arrays, 4, 8, 128)
+    vmem(f"{key}_high", arrays, 4, 8, 128)
+    vmem(f"{key}_zed", arrays, 8, 128)
+    vmem(f"{key}_xr", 2, arrays, 5, 8, 128)
+    vmem(f"{key}_yr", 6, arrays, 4, 8, 128)
+    vmem(f"{key}_zr", 18, arrays, 8, 128)
+    vmem(f"{key}_ext", arrays, 17 * 16, 128)
+    dma(f"{key}_ss", 26)
+    dma(f"{key}_rs", 26)
+vmem("a1_snd", 8, 128)
+vmem("a1_rcv", 8, 128)
+dma("a1_ss", 1)
+dma("a1_rs", 1)
+vmem("lyp1", 8 * 16, 128)
+vmem("q1", 8 * 16, 128)
+vmem("h1", 6, 8, 128)
+for key, rows, count in (("a0", 16, 3), ("b", 16, 6), ("c", 16, 6), ("h", 16, 6)):
     vmem(f"{key}_snd", count, rows, 128)
     vmem(f"{key}_rcv", count, rows, 128)
     dma(f"{key}_ss", count)
@@ -103,9 +125,14 @@
     dma(f"{key}_ss", 11)
     dma(f"{key}_rs", 11)
 for key in ("f2", "lx2", "ly2", "lz2", "va2", "vb2"):
-    vmem(key, 36, 16, 128)
+    vmem(key, 2, 20, 16, 128)
 for key in ("cxl2", "cxu2", "cyl2", "cyu2", "czl2", "czu2", "g2", "d152", "kw2"):
-    vmem(key, 36, 16, 128)
+    vmem(key, 2, 20, 16, 128)
+for key, arrays in (("nf", 3), ("nv", 1)):
+    vmem(f"{key}_snd", arrays, 2, 8, 8, 128)
+    vmem(f"{key}_rcv", 2, arrays, 2, 8, 8, 128)
+    dma(f"{key}_ss", 2)
+    dma(f"{key}_rs", 2)
 vmem("s2", 128, 128)
 vmem("p2", 256, 128)
 vmem("face3", 3, 128, 128)
@@ -122,8 +149,6 @@
 vmem("fc4", 3, 32, 128)
 for key in ("t5", "cx5", "cyl5", "cyu5", "czl5", "czu5", "kw5", "e5"):
     vmem(key, 8, 128)
-vmem("q1", 96, 128)
-vmem("h1", 6, 8, 128)
 
 
 class Space:
@@ -153,8 +178,8 @@
         load.start()
 
     barrier = pltpu.get_barrier_semaphore()
-    friends = list(dict.fromkeys(RING_Y + RING_Z + PLANE))
-    friends = list(dict.fromkeys((x & 3, y & 7, z & 7) for x, y, z in friends))
+    friends = [(x & 3, y & 7, z & 7) for x, y, z in RING_Z + AROUND]
+    friends = list(dict.fromkeys(friends))
     for offset in friends:
         pl.semaphore_signal(barrier, inc=1, device_id=peer(offset), device_id_type=MESH)
 
@@ -187,10 +212,10 @@
     top_x, top_y, top_z = flag(gx < GX - 1), flag(gy < GY - 1), flag(gz < GZ - 1)
 
 
-    def pack(read, block, column):
-        packed = jnp.zeros((block.Y, 128), F32)
-        lane = lanes(block.Y)
-        for i in range(block.X):
+    def pack(read, rows, count, column):
+        packed = jnp.zeros((rows, 128), F32)
+        lane = lanes(rows)
+        for i in range(count):
             packed = jnp.where(lane == i, turn(read(i), i - column), packed)
         return packed
 
@@ -200,8 +225,8 @@
         snd[1] = ref[block.at(0)]
         snd[2] = ref[block.row_of_each(block.Y - 1)]
         snd[3] = ref[block.row_of_each(0)]
-        snd[4] = pack(lambda i: ref[block.at(i)], block, block.Z - 1)
-        snd[5] = pack(lambda i: ref[block.at(i)], block, 0)
+        snd[4] = pack(lambda i: ref[block.at(i)], 16, 16, 127)
+        snd[5] = pack(lambda i: ref[block.at(i)], 16, 16, 0)
         rcv = getattr(s, key + "_rcv")
         return copies(
             FACES,
@@ -217,12 +242,12 @@
         ref[block.row_of_each(-1)] = halo[2]
         ref[block.row_of_each(block.Y)] = halo[3]
 
-    def send_upper(level, lx, ly, lz, key):
-        block = BLOCKS[level]
+    def send_upper(lx, ly, lz, key):
+        block = B0
         snd = getattr(s, key + "_snd")
         snd[0] = lx[block.own(0)]
         snd[1] = ly[pl.ds(0, block.X, stride=block.Y)]
-        snd[2] = pack(lambda i: lz[block.own(i)], block, 0)
+        snd[2] = pack(lambda i: lz[block.own(i)], 16, 16, 0)
         rcv = getattr(s, key + "_rcv")
         return copies(
             DOWN,
@@ -233,7 +258,7 @@
         )
 
     def coefficients(level, lx, ly, lz, key):
-        block = BLOCKS[level]
+        block = B0
         rcv = getattr(s, key + "_rcv")
         lyp = getattr(s, f"lyp{level}")
         c = {k: getattr(s, f"{k}{level}") for k in ("cxl", "cxu", "cyl", "cyu", "czl", "czu")}
@@ -268,7 +293,7 @@
             c["czu"][own] = scale * a_zu
 
     def stencil(level, ref, low, high, emit):
-        block = BLOCKS[level]
+        block = B0
         lane = lanes(block.Y)
         get = lambda k: getattr(s, f"{k}{level}")
         for i in range(block.X):
@@ -282,7 +307,7 @@
             emit(i, v, get("g")[own] + (t_x + t_y + t_z))
 
     def smooth(level, source, target, low, high):
-        block = BLOCKS[level]
+        block = B0
 
         def emit(i, v, total):
             target[block.at(i)] = v * THIRD + total
@@ -290,7 +315,7 @@
         stencil(level, source, low, high, emit)
 
     def residual(level, source, low, high):
-        block = BLOCKS[level]
+        block = B0
         d15, r = getattr(s, f"d15{level}"), getattr(s, f"r{level}")
 
         def emit(i, v, total):
@@ -298,7 +323,133 @@
 
         stencil(level, source, low, high, emit)
 
+
     lane8, lane16 = lanes(8), lanes(16)
+    row8, row16 = sublanes(8), sublanes(16)
+    upper_half = row8 < 4
+    slices_x = {1: (4, 4), -1: (0, 5), 0: (0, 8)}
+    pairs_x = {1: (2, 2), -1: (0, 3), 0: (0, 4)}
+    flat_yr = [(x, y) for x in (1, -1, 0) for y in (1, -1)]
+    flat_zr = [(x, y, z) for x in (1, -1, 0) for y in (1, -1, 0) for z in (1, -1)]
+
+    def send_around(arrays, key):
+        get = lambda name: getattr(s, f"{key}_{name}")
+        own, low, high, zed = get("own"), get("low"), get("high"), get("zed")
+        for a in range(arrays):
+            for i in range(4):
+                even, odd = own[a, 2 * i], own[a, 2 * i + 1]
+                low[a, i] = jnp.where(upper_half, even, turn(odd, 4, 0))
+                high[a, i] = jnp.where(upper_half, turn(even, 4, 0), odd)
+            packed = jnp.zeros((8, 128), F32)
+            for x in range(8):
+                v = own[a, x]
+                packed = jnp.where((lane8 >> 3) == 2 * x, turn(v, 16 * x), packed)
+                packed = jnp.where((lane8 >> 3) == 2 * x + 1, turn(v, 16 * x - 48), packed)
+            zed[a] = packed
+
+        def source(k):
+            x, y, z = AROUND[k]
+            if z != 0:
+                return zed
+            if y != 0:
+                first, count = pairs_x[x]
+                return (low if y < 0 else high).at[:, pl.ds(first, count)]
+            first, count = slices_x[x]
+            return own.at[:, pl.ds(first, count)]
+
+        def target(k):
+            x, y, z = AROUND[k]
+            if z != 0:
+                return get("zr").at[flat_zr.index((x, y, z))]
+            if y != 0:
+                return get("yr").at[flat_yr.index((x, y)), :, pl.ds(0, pairs_x[x][1])]
+            return get("xr").at[0 if x > 0 else 1, :, pl.ds(0, slices_x[x][1])]
+
+        return copies(AROUND, source, target, get("ss"), get("rs"))
+
+    def assemble(arrays, key):
+        get = lambda name: getattr(s, f"{key}_{name}")
+        own, xr, yr, zr, ext = get("own"), get("xr"), get("yr"), get("zr"), get("ext")
+        first8 = (lane8 & 15) < 8
+        side_high, side_low = (lane16 >= 64) & (lane16 < 72), lane16 >= 120
+
+        def zed(a, x, y):
+            above = zr[flat_zr.index((x, y, -1)), a]
+            below = zr[flat_zr.index((x, y, 1)), a]
+            return jnp.where(first8, above, below)
+
+        for a in range(arrays):
+            combs = {}
+            for x in (1, -1, 0):
+                outer = jnp.where(upper_half, zed(a, x, -1), zed(a, x, 1))
+                combs[x] = jnp.concatenate([zed(a, x, 0), outer], axis=0)
+            for k in range(17):
+                x = k - 4
+                if x < 0:
+                    d, layer, place = 1, x + 4, x + 8
+                elif x < 8:
+                    d, layer, place = 0, x, x
+                else:
+                    d, layer, place = -1, x - 8, x - 8
+                inner = own[a, layer] if d == 0 else xr[0 if d > 0 else 1, a, layer]
+                above = yr[flat_yr.index((d, -1)), a, layer // 2]
+                below = yr[flat_yr.index((d, 1)), a, layer // 2]
+                if layer % 2 == 0:
+                    below = turn(below, 4, 0)
+                else:
+                    above = turn(above, 4, 0)
+                outer = jnp.where(upper_half, above, below)
+                whole = jnp.concatenate([inner, outer], axis=0)
+                comb = combs[d]
+                whole = jnp.where(side_high, turn(comb, 64 - 16 * place), whole)
+                whole = jnp.where(side_low, turn(comb, 112 - 16 * place), whole)
+                ext[a, pl.ds(16 * k, 16)] = whole
+
+    def ext1(k):
+        return pl.ds(16 * k, 16)
+
+    def pad1(k):
+        return pl.ds(16 * k + 16, 16)
+
+    def coefficients1():
+        keep_y = jnp.where(row16 == 0, low_y, 1.0)
+        keep_z = jnp.where(lane16 == 0, low_z, 1.0)
+        last_z = jnp.where(lane16 == 63, top_z, 1.0)
+        for k in range(16):
+            own = ext1(k)
+            a_xl, a_yl, a_zl = s.hf_ext[0, own], s.hf_ext[1, own], s.hf_ext[2, own]
+            a_xu = s.hf_ext[0, ext1(k + 1)]
+            if k == 11:
+                a_xu = a_xu * top_x
+            a_yu = s.hf_ext[3, own]
+            a_zu = turn(a_zl, -1) * last_z
+            total = (a_xl + a_yl + a_zl) + (a_xu + a_yu + a_zu)
+            scale = RELAX / total
+            s.kw1[own] = scale * 4.0
+            if 1 <= k <= 14:
+                s.d151[own] = (1.5 * 0.25) * total
+                s.cxl1[own] = scale * a_xl * (low_x if k == 4 else 1.0)
+                s.cxu1[own] = scale * a_xu
+                s.cyl1[own] = scale * a_yl * keep_y
+                s.cyu1[own] = scale * a_yu
+                s.czl1[own] = scale * a_zl * keep_z
+                s.czu1[own] = scale * a_zu
+
+    def stencil1(first, last, ref, emit):
+        for k in range(first, last + 1):
+            own = ext1(k)
+            v = ref[pad1(k)]
+            t_x = s.cxl1[own] * ref[pad1(k - 1)] + s.cxu1[own] * ref[pad1(k + 1)]
+            t_y = s.cyl1[own] * turn(v, 1, 0) + s.cyu1[own] * turn(v, -1, 0)
+            t_z = s.czl1[own] * turn(v, 1) + s.czu1[own] * turn(v, -1)
+            emit(k, v, s.g1[own] + (t_x + t_y + t_z))
+
+    def smooth1(first, last, source, target):
+        def emit(k, v, total):
+            target[pad1(k)] = v * THIRD + total
+
+        stencil1(first, last, source, emit)
+
     even8 = (2 * lane8) & 127
     half16 = lane16 >> 1
 
@@ -343,18 +494,25 @@
     s.t16[0] = pair_z(s.t16[0]) * 0.25
     s.t16[1] = pair_z(s.t16[1]) * 0.25
     stage_z(3, s.zf_snd)
-    for ref in (s.va0, s.vb0, s.va1, s.vb1):
-        ref[...] = jnp.zeros_like(ref)
-    for ref in (s.lx2, s.ly2, s.lz2):
-        ref[...] = jnp.ones_like(ref)
-    for ref in (s.f2, s.va2, s.vb2):
-        ref[...] = jnp.zeros_like(ref)
-    for ref in (s.va3, s.vb3, s.p2):
-        ref[...] = jnp.zeros_like(ref)
+    for ref in (s.va1, s.vb1):
+        for k in (-1, 17):
+            ref[pad1(k)] = jnp.zeros((16, 128), F32)
+    for p in range(2):
+        for x in (0, 1, 18, 19):
+            for ref in (s.va2, s.vb2):
+                ref[p, x] = jnp.zeros((16, 128), F32)
+        for x in range(16):
+            s.f2[p, x + 2] = jnp.zeros((16, 128), F32)
+    for ref in (s.va3, s.vb3):
+        for k in range(2):
+            ref[pl.ds(8 * k, 8)] = jnp.zeros((8, 128), F32)
+            ref[pl.ds(144 + 8 * k, 8)] = jnp.zeros((8, 128), F32)
+    s.p2[...] = jnp.zeros_like(s.p2)
+    s.a1_snd[...] = s.fy1[pl.ds(0, 8, stride=8)]
 
     pl.semaphore_wait(barrier, len(friends))
-    round_a0 = send_upper(0, s.fx, s.fy, s.fz, "a0")
-    round_a1 = send_upper(1, s.fx1, s.fy1, s.fz1, "a1")
+    round_a0 = send_upper(s.fx, s.fy, s.fz, "a0")
+    round_a1 = copies([DOWN[1]], lambda k: s.a1_snd, lambda k: s.a1_rcv, s.a1_ss, s.a1_rs)
     round_zf = copies(
         RING_Z, lambda k: s.zf_snd, lambda k: s.zf_rcv.at[k], s.zf_ss, s.zf_rs
     )
@@ -368,41 +526,46 @@
         s.va0[B0.at(i)] = start
     round_b = send_faces(B0, s.va0, "b")
     finish(round_a1)
-    coefficients(1, s.fx1, s.fy1, s.fz1, "a1")
+    for i in range(8):
+        s.lyp1[pl.ds(16 * i, 8)] = s.fy1[pl.ds(8 * i, 8)]
+    s.lyp1[pl.ds(8, 8, stride=16)] = s.a1_rcv[...] * top_y
+    for i in range(8):
+        own = pl.ds(8 * i, 8)
+        s.hf_own[0, i] = s.fx1[own]
+        s.hf_own[1, i] = s.fy1[own]
+        s.hf_own[2, i] = s.fz1[own]
+        s.hf_own[3, i] = s.lyp1[pl.ds(16 * i + 1, 8)]
     finish(round_b)
     fill(B0, s.va0, s.b_rcv)
     smooth(0, s.va0, s.vb0, s.b_rcv[4], s.b_rcv[5])
     round_c = send_faces(B0, s.vb0, "c")
+    round_hf = send_around(4, "hf")
     finish(round_zf)
     merge_z(3, s.zf_snd, s.zf_rcv, s.xf_snd)
+    round_xf = copies(
+        LINE, lambda k: s.xf_snd, lambda k: s.xf_rcv.at[k], s.xf_ss, s.xf_rs
+    )
     finish(round_c)
-    round_xf = copies(
-        PLANE, lambda k: s.xf_snd, lambda k: s.xf_rcv.at[k], s.xf_ss, s.xf_rs
-    )
     fill(B0, s.vb0, s.c_rcv)
     residual(0, s.vb0, s.c_rcv[4], s.c_rcv[5])
 
     for i in range(8):
-        own = pl.ds(8 * i, 8)
         here = lambda shift: s.r0[pl.ds(32 * i + shift, 8, stride=2)]
         total = (here(0) + here(1)) + (here(16) + here(17))
-        start = s.kw1[own] * (take(pair_z(total), even8) * 0.125)
-        s.g1[own] = start
-        s.va1[B1.at(i)] = start
-    round_d = send_faces(B1, s.va1, "d")
-    finish(round_d)
-    fill(B1, s.va1, s.d_rcv)
-    smooth(1, s.va1, s.vb1, s.d_rcv[4], s.d_rcv[5])
-    round_e = send_faces(B1, s.vb1, "e")
+        s.hr_own[0, i] = take(pair_z(total), even8) * 0.125
+    round_hr = send_around(1, "hr")
+    finish(round_hf)
+    assemble(4, "hf")
+    coefficients1()
 
 
     def block2(p, x):
-        return 18 * p + 1 + x
-
-    def spread(arrays, snd, rcv, targets):
+        return (p, x + 2)
+
+    def spread(arrays, offsets, snd, rcv, targets):
         parts = [((0, 0, 0), lambda q: snd.at[q])]
-        for k in range(11):
-            parts.append((PLANE[k], lambda q, k=k: rcv.at[k, q]))
+        for k, offset in enumerate(offsets):
+            parts.append((offset, lambda q, k=k: rcv.at[k, q]))
         for offset, part in parts:
             first = 4 * ((gx - offset[0]) & 3)
             place = pl.ds(4 * (1 - offset[1]), 4)
@@ -410,13 +573,67 @@
                 for p in range(2):
                     for x in range(4):
                         piece = part(2 * a + p)[pl.ds(4 * x, 4)]
-                        targets[a][block2(p, x) + first, place] = piece
-
+                        targets[a][p, x + 2 + first, place] = piece
+
+    def send_sides(refs, key):
+        snd, rcv = getattr(s, key + "_snd"), getattr(s, key + "_rcv")
+        for a, ref in enumerate(refs):
+            for p in range(2):
+                for i in range(8):
+                    even = ref[p, 2 * i + 2, pl.ds(0, 8)]
+                    odd = ref[p, 2 * i + 3, pl.ds(0, 8)]
+                    snd[a, p, i] = jnp.where(upper_half, turn(even, 4, 0), odd)
+        return copies(
+            SIDES,
+            lambda k: snd,
+            lambda k: rcv.at[k],
+            getattr(s, key + "_ss"),
+            getattr(s, key + "_rs"),
+        )
+
+    def take_sides(refs, key, rest):
+        rcv = getattr(s, key + "_rcv")
+        for a, ref in enumerate(refs):
+            for p in range(2):
+                for x in range(16):
+                    below, above = rcv[0, a, p, x // 2], rcv[1, a, p, x // 2]
+                    if x % 2 == 1:
+                        below, above = turn(below, 4, 0), turn(above, 4, 0)
+                    own = ref[p, x + 2, pl.ds(0, 8)]
+                    ref[p, x + 2, pl.ds(0, 8)] = jnp.where(upper_half, below, own)
+                    ref[p, x + 2, pl.ds(8, 8)] = jnp.where(upper_half, above, rest)
+
+    faces2 = (s.lx2, s.ly2, s.lz2)
     finish(round_xf)
-    spread(3, s.xf_snd, s.xf_rcv, (s.lx2, s.ly2, s.lz2))
-    row16 = sublanes(16)
+    spread(3, LINE, s.xf_snd, s.xf_rcv, faces2)
+    round_nf = send_sides(faces2, "nf")
     global_y = row16 + 4 * gy - 4
     not_low, not_top = global_y != 0, global_y != 4 * GY - 1
+
+    finish(round_hr)
+    assemble(1, "hr")
+    for k in range(16):
+        start = s.kw1[ext1(k)] * s.hr_ext[0, ext1(k)]
+        s.g1[ext1(k)] = start
+        s.va1[pad1(k)] = start
+    smooth1(1, 14, s.va1, s.vb1)
+
+    def emit_r1(k, v, total):
+        r = s.d151[ext1(k)] * (total - RELAX * v)
+        s.r1[pl.ds(8 * (k - 4), 8)] = r[0:8]
+
+    stencil1(4, 11, s.vb1, emit_r1)
+    for i in range(4):
+        here = lambda shift: s.r1[pl.ds(16 * i + shift, 4, stride=2)]
+        s.t16[0, pl.ds(4 * i, 4)] = (here(0) + here(1)) + (here(8) + here(9))
+    s.t16[0] = pair_z(s.t16[0]) * 0.125
+    stage_z(1, s.zr_snd)
+    round_zr = copies(
+        RING_Z, lambda k: s.zr_snd, lambda k: s.zr_rcv.at[k], s.zr_ss, s.zr_rs
+    )
+
+    finish(round_nf)
+    take_sides(faces2, "nf", 1.0)
 
     for a, ref in enumerate((s.lx2, s.ly2, s.lz2)):
         for i in range(8):
@@ -446,7 +663,7 @@
         for x in range(16):
             j = block2(p, x)
             a_xl, a_yl, a_zl = s.lx2[j], s.ly2[j], s.lz2[j]
-            a_xu = s.lx2[j + 1] if x < 15 else jnp.zeros((16, 128), F32)
+            a_xu = s.lx2[block2(p, x + 1)] if x < 15 else jnp.zeros((16, 128), F32)
             a_yu = jnp.where(not_top, turn(a_yl, -1, 0), 0.0)
             if p == 0:
                 a_zu = s.lz2[block2(1, x)]
@@ -468,7 +685,7 @@
             for x in range(16):
                 j, other = block2(p, x), block2(1 - p, x)
                 v, w = ref[j], ref[other]
-                t_x = s.cxl2[j] * ref[j - 1] + s.cxu2[j] * ref[j + 1]
+                t_x = s.cxl2[j] * ref[block2(p, x - 1)] + s.cxu2[j] * ref[block2(p, x + 1)]
                 t_y = s.cyl2[j] * turn(v, 1, 0) + s.cyu2[j] * turn(v, -1, 0)
                 down, up = (turn(w, 1), w) if p == 0 else (w, turn(w, -1))
                 t_z = s.czl2[j] * down + s.czu2[j] * up
@@ -480,20 +697,13 @@
 
         stencil2(source, emit)
 
-    finish(round_e)
-    fill(B1, s.vb1, s.e_rcv)
-    residual(1, s.vb1, s.e_rcv[4], s.e_rcv[5])
-    for i in range(4):
-        here = lambda shift: s.r1[pl.ds(16 * i + shift, 4, stride=2)]
-        s.t16[0, pl.ds(4 * i, 4)] = (here(0) + here(1)) + (here(8) + here(9))
-    s.t16[0] = pair_z(s.t16[0]) * 0.125
-    stage_z(1, s.zr_snd)
-    round_zr = copies(
-        RING_Z, lambda k: s.zr_snd, lambda k: s.zr_rcv.at[k], s.zr_ss, s.zr_rs
+    finish(round_zr)
+    merge_z(1, s.zr_snd, s.zr_rcv, s.xr_snd)
+    round_xr = copies(
+        PLANE, lambda k: s.xr_snd, lambda k: s.xr_rcv.at[k], s.xr_ss, s.xr_rs
     )
 
     finish(round_yf)
-    row8 = sublanes(8)
     zero8 = jnp.zeros((8, 128), F32)
     for y in range(16):
         own = pl.ds(8 * y, 8)
@@ -577,13 +787,8 @@
     s.czl5[...] = jnp.where(lane8 < 4, 0.0, scale * a_zl)
     s.czu5[...] = scale * a_zu
 
-    finish(round_zr)
-    merge_z(1, s.zr_snd, s.zr_rcv, s.xr_snd)
-    round_xr = copies(
-        PLANE, lambda k: s.xr_snd, lambda k: s.xr_rcv.at[k], s.xr_ss, s.xr_rs
-    )
     finish(round_xr)
-    spread(1, s.xr_snd, s.xr_rcv, (s.f2,))
+    spread(1, PLANE, s.xr_snd, s.xr_rcv, (s.f2,))
     for p in range(2):
         for x in range(16):
             j = block2(p, x)
@@ -607,6 +812,7 @@
     round_yr = copies(
         RING_Y, lambda k: s.f3.at[mine], lambda k: s.f3.at[mine], s.yr_ss, s.yr_rs
     )
+    round_nv = send_sides((s.vb2,), "nv")
     finish(round_yr)
 
     def at3(y):
@@ -683,6 +889,8 @@
     smooth3(s.vb3, s.va3)
     smooth3(s.va3, s.vb3)
 
+    finish(round_nv)
+    take_sides((s.vb2,), "nv", 0.0)
     for k in range(6):
         piece = s.vb3[pl.ds(pl.multiple_of(16 * gy + 8 * k, 8), 8)]
         for x in range(2):
@@ -698,33 +906,25 @@
     signed = jnp.where(lane16 < 96, lane16, lane16 - 128)
     index = (16 * gz + (signed >> 2)) & 127
     odd = ((signed >> 1) & 1) == 1
-    for k in range(6):
-        x = 4 * gx + k - 1
-        s.q1[pl.ds(16 * k, 16)] = jnp.where(
-            odd, take(s.vb2[block2(1, x)], index), take(s.vb2[block2(0, x)], index)
-        )
-    for k, source in ((0, 0), (1, 5)):
+    for k in range(8):
+        x = 4 * gx + k
+        piece = jnp.where(odd, take(s.vb2[1, x], index), take(s.vb2[0, x], index))
+        rows = jnp.where(row16 < 6, turn(piece, -4, 0), turn(piece, 4, 0))[0:8]
         for y in range(2):
-            s.h1[k, pl.ds(y, 4, stride=2)] = s.q1[pl.ds(16 * source + 4, 4)]
-    for k, source in ((2, 3), (3, 8)):
-        for x in range(2):
-            s.h1[k, pl.ds(x, 4, stride=2)] = s.q1[pl.ds(16 + source, 4, stride=16)]
-    for i in range(8):
-        for y in range(2):
-            s.w1[pl.ds(8 * i + y, 4, stride=2)] = s.q1[pl.ds(16 * (i // 2 + 1) + 4, 4)]
-    s.h1[4] = pack(lambda i: s.w1[B1.own(i)], B1, 127)
-    s.h1[5] = pack(lambda i: s.w1[B1.own(i)], B1, 64)
-    for k in range(6):
-        s.h1[k] = s.h1[k] + s.e_rcv[k]
-    for i in range(8):
-        s.vb1[B1.at(i)] = s.vb1[B1.at(i)] + s.w1[B1.own(i)]
-    fill(B1, s.vb1, s.h1)
-    smooth(1, s.vb1, s.va1, s.h1[4], s.h1[5])
-    round_f = send_faces(B1, s.va1, "f")
-    finish(round_f)
-    fill(B1, s.va1, s.f_rcv)
-    smooth(1, s.va1, s.vb1, s.f_rcv[4], s.f_rcv[5])
-    round_q = send_faces(B1, s.vb1, "q")
+            s.q1[pl.ds(16 * k + y, 8, stride=2)] = rows
+        more = s.q1[pl.ds(16 * k, 16)]
+        for i in (2 * k, 2 * k + 1):
+            if 1 <= i <= 14:
+                s.vb1[pad1(i)] = s.vb1[pad1(i)] + more
+    smooth1(2, 13, s.vb1, s.va1)
+    smooth1(3, 12, s.va1, s.vb1)
+    s.h1[0] = s.vb1[pl.ds(16 * 4, 8)]
+    s.h1[1] = s.vb1[pl.ds(16 * 13, 8)]
+    s.h1[2] = s.vb1[pl.ds(16 * 5 + 15, 8, stride=16)]
+    s.h1[3] = s.vb1[pl.ds(16 * 5 + 8, 8, stride=16)]
+    inner = lambda i: s.vb1[pl.ds(16 * (i + 5), 8)]
+    s.h1[4] = pack(inner, 8, 8, 127)
+    s.h1[5] = pack(inner, 8, 8, 64)
 
     def widen(value, ref, start):
         ref[pl.ds(start, 8, stride=2)] = value
@@ -732,12 +932,11 @@
         return take(ref[pl.ds(start, 16)], half16)
 
     for i in range(8):
-        more = widen(s.vb1[B1.at(i)], s.w0, 16 * i)
+        more = widen(inner(i), s.w0, 16 * i)
         for x in (2 * i, 2 * i + 1):
             s.vb0[B0.at(x)] = s.vb0[B0.at(x)] + more
-    finish(round_q)
     for k in range(6):
-        s.c_rcv[k] = s.c_rcv[k] + widen(s.q_rcv[k], s.w0, 128 + 16 * k)
+        s.c_rcv[k] = s.c_rcv[k] + widen(s.h1[k], s.w0, 128 + 16 * k)
     fill(B0, s.vb0, s.c_rcv)
     smooth(0, s.vb0, s.va0, s.c_rcv[4], s.c_rcv[5])
     round_h = send_faces(B0, s.va0, "h")
@@ -755,7 +954,7 @@
     whole = pl.pallas_call(
         cycle,
         out_shape=jax.ShapeDtypeStruct((256, 128), F32),
-        in_specs=[pl.BlockSpec(memory_space=pl.ANY)] * 4,
+        in_specs=[pl.BlockSpec(memory_space=pltpu.HBM)] * 4,
         out_specs=pl.BlockSpec(memory_space=pltpu.VMEM),
         scratch_shapes=list(SCRATCH.values()),
         compiler_params=pltpu.CompilerParams(

time: 66.4 us -> 61.3 us (0.923)
  Pallas kernels: 62 us -> 56.6 us
    pallas_call x1, Pallas kernels: 62 us -> 56.6 us  [shards(): pl.pallas_call(cycle, out_shape=jax.ShapeDtypeStruct((256, 128), F32), in...]
where the time goes in v1:
time: 61.3 us; the launch traced here: 60.9 us
  Pallas kernels  56.6 us (92%)
  local copies, waits for them, and re-layouts  4.27 us (7%)
    pallas_call x1, Pallas kernels, shards(): pl.pallas_call(cycle, out_shape=jax.ShapeDtypeStruct((256, 128), F32), in...  56.6 us
    unnamed x9, local copies, waits for them, and re-layouts  4.27 us

profile of v1, /device:TPU:1, one launch (start us, length us, event | category | flops | bytes accessed | tf_op | source)
XLA Modules:
  0.0 60.9 jit_solution(14821513397027648343)
XLA Ops:
  0.0 0.0 copy-start
  0.0 0.9 %copy-done = f32[16,16,128]{2,1,0:T(8,128)S(1)} copy-done((f32[16,16,128]{2,1,0:T(8,128)S(1)}, f32[16,16,128]{2,1,0:T(8,128)}, u32[]{:S(2)}) %copy-start) | copy-done | bytes 131096
  0.9 0.0 copy-start.1
  0.9 0.9 %copy-done.1 = f32[16,16,128]{2,1,0:T(8,128)S(1)} copy-done((f32[16,16,128]{2,1,0:T(8,128)S(1)}, f32[16,16,128]{2,1,0:T(8,128)}, u32[]{:S(2)}) %copy-start.1) | copy-done | bytes 131096
  1.8 0.0 copy-start.2
  1.8 0.9 %copy-done.2 = f32[16,16,128]{2,1,0:T(8,128)S(1)} copy-done((f32[16,16,128]{2,1,0:T(8,128)S(1)}, f32[16,16,128]{2,1,0:T(8,128)}, u32[]{:S(2)}) %copy-start.2) | copy-done | bytes 131096
  2.7 0.0 copy-start.3
  2.7 0.9 %copy-done.3 = f32[16,16,128]{2,1,0:T(8,128)S(1)} copy-done((f32[16,16,128]{2,1,0:T(8,128)S(1)}, f32[16,16,128]{2,1,0:T(8,128)}, u32[]{:S(2)}) %copy-start.3) | copy-done | bytes 131096
  3.6 56.6 %vcycle.1 = f32[256,128]{1,0:T(8,128)S(1)} custom-call(f32[256,128]{1,0:T(8,128)S(1)} %bitcast.6, f32[256,128]{1,0:T(8,128)S(1)} %bitcast.7, f32[256,128]{1,0:T(8,128)S(1)} %bitcast.8, f32[256,128]{1,0:T(8,128)S(1)} %bitcast.9), custom_call_target="tpu_custom_call" | custom-call | tf_op jit(solution)/shard_map/vcycle/pallas_call | solution.py:954
  60.2 0.7 %copy.6 = f32[16,16,128]{2,1,0:T(8,128)} copy(f32[16,16,128]{2,1,0:T(8,128)S(1)} %bitcast.5) | data formatting | bytes 262144
Async XLA Ops:
  0.0 0.9 %copy-start = (f32[16,16,128]{2,1,0:T(8,128)S(1)}, f32[16,16,128]{2,1,0:T(8,128)}, u32[]{:S(2)}) copy-start(f32[16,16,128]{2,1,0:T(8,128)} %param.4) | copy-start | bytes 393220
  0.9 0.9 %copy-start.1 = (f32[16,16,128]{2,1,0:T(8,128)S(1)}, f32[16,16,128]{2,1,0:T(8,128)}, u32[]{:S(2)}) copy-start(f32[16,16,128]{2,1,0:T(8,128)} %param.5) | copy-start | bytes 393220
  1.8 0.9 %copy-start.2 = (f32[16,16,128]{2,1,0:T(8,128)S(1)}, f32[16,16,128]{2,1,0:T(8,128)}, u32[]{:S(2)}) copy-start(f32[16,16,128]{2,1,0:T(8,128)} %param.6) | copy-start | bytes 393220
  2.7 0.9 %copy-start.3 = (f32[16,16,128]{2,1,0:T(8,128)S(1)}, f32[16,16,128]{2,1,0:T(8,128)}, u32[]{:S(2)}) copy-start(f32[16,16,128]{2,1,0:T(8,128)} %param.7) | copy-start | bytes 393220

commit v2 on v1

--- a/solution.py
+++ b/solution.py
@@ -90,25 +90,19 @@
     vmem(key, 17 * 16, 128)
 for key in ("va1", "vb1"):
     vmem(key, 19 * 16, 128)
-for key, arrays in (("hf", 4), ("hr", 1)):
-    vmem(f"{key}_own", arrays, 8, 8, 128)
-    vmem(f"{key}_low", arrays, 4, 8, 128)
-    vmem(f"{key}_high", arrays, 4, 8, 128)
-    vmem(f"{key}_zed", arrays, 8, 128)
-    vmem(f"{key}_xr", 2, arrays, 5, 8, 128)
-    vmem(f"{key}_yr", 6, arrays, 4, 8, 128)
-    vmem(f"{key}_zr", 18, arrays, 8, 128)
-    vmem(f"{key}_ext", arrays, 17 * 16, 128)
-    dma(f"{key}_ss", 26)
-    dma(f"{key}_rs", 26)
-vmem("a1_snd", 8, 128)
-vmem("a1_rcv", 8, 128)
-dma("a1_ss", 1)
-dma("a1_rs", 1)
-vmem("lyp1", 8 * 16, 128)
+vmem("ext1", 4, 17 * 16, 128)
+vmem("hw_own", 5, 8, 8, 128)
+vmem("hw_low", 5, 4, 8, 128)
+vmem("hw_high", 5, 4, 8, 128)
+vmem("hw_zed", 2, 8, 128)
+vmem("hw_xr", 2, 5, 3, 8, 128)
+vmem("hw_yr", 6, 5, 4, 8, 128)
+vmem("hw_zr", 18, 8, 128)
+dma("hw_ss", 26)
+dma("hw_rs", 26)
 vmem("q1", 8 * 16, 128)
 vmem("h1", 6, 8, 128)
-for key, rows, count in (("a0", 16, 3), ("b", 16, 6), ("c", 16, 6), ("h", 16, 6)):
+for key, rows, count in (("a0", 16, 3), ("b", 16, 6), ("c", 16, 6), ("h", 16, 6), ("a1", 8, 3), ("d", 8, 6), ("e", 8, 6)):
     vmem(f"{key}_snd", count, rows, 128)
     vmem(f"{key}_rcv", count, rows, 128)
     dma(f"{key}_ss", count)
@@ -178,9 +172,7 @@
         load.start()
 
     barrier = pltpu.get_barrier_semaphore()
-    friends = [(x & 3, y & 7, z & 7) for x, y, z in RING_Z + AROUND]
-    friends = list(dict.fromkeys(friends))
-    for offset in friends:
+    for offset in FACES:
         pl.semaphore_signal(barrier, inc=1, device_id=peer(offset), device_id_type=MESH)
 
     def copies(offsets, sources, targets, ss, rs):
@@ -249,6 +241,7 @@
         snd[1] = ly[pl.ds(0, block.X, stride=block.Y)]
         snd[2] = pack(lambda i: lz[block.own(i)], 16, 16, 0)
         rcv = getattr(s, key + "_rcv")
+        pl.semaphore_wait(barrier, len(FACES))
         return copies(
             DOWN,
             lambda k: snd.at[k],
@@ -327,83 +320,72 @@
     lane8, lane16 = lanes(8), lanes(16)
     row8, row16 = sublanes(8), sublanes(16)
     upper_half = row8 < 4
-    slices_x = {1: (4, 4), -1: (0, 5), 0: (0, 8)}
-    pairs_x = {1: (2, 2), -1: (0, 3), 0: (0, 4)}
+    slices_x = {1: (5, 3), -1: (0, 3), 0: (0, 8)}
+    pairs_x = {1: (2, 2), -1: (0, 2), 0: (0, 4)}
     flat_yr = [(x, y) for x in (1, -1, 0) for y in (1, -1)]
     flat_zr = [(x, y, z) for x in (1, -1, 0) for y in (1, -1, 0) for z in (1, -1)]
 
-    def send_around(arrays, key):
-        get = lambda name: getattr(s, f"{key}_{name}")
-        own, low, high, zed = get("own"), get("low"), get("high"), get("zed")
-        for a in range(arrays):
+    def send_around():
+        zeds = [jnp.zeros((8, 128), F32)] * 2
+        group = lane8 // 3
+        for a in range(5):
             for i in range(4):
-                even, odd = own[a, 2 * i], own[a, 2 * i + 1]
-                low[a, i] = jnp.where(upper_half, even, turn(odd, 4, 0))
-                high[a, i] = jnp.where(upper_half, turn(even, 4, 0), odd)
-            packed = jnp.zeros((8, 128), F32)
+                even, odd = s.hw_own[a, 2 * i], s.hw_own[a, 2 * i + 1]
+                s.hw_low[a, i] = jnp.where(upper_half, even, turn(odd, 4, 0))
+                s.hw_high[a, i] = jnp.where(upper_half, turn(even, 4, 0), odd)
             for x in range(8):
-                v = own[a, x]
-                packed = jnp.where((lane8 >> 3) == 2 * x, turn(v, 16 * x), packed)
-                packed = jnp.where((lane8 >> 3) == 2 * x + 1, turn(v, 16 * x - 48), packed)
-            zed[a] = packed
+                v, place = s.hw_own[a, x], 8 * a + x
+                zeds = [
+                    jnp.where(group == place, turn(v, 3 * place - first), zed)
+                    for zed, first in zip(zeds, (61, 0))
+                ]
+        s.hw_zed[0], s.hw_zed[1] = zeds
 
         def source(k):
             x, y, z = AROUND[k]
             if z != 0:
-                return zed
+                return s.hw_zed.at[0 if z > 0 else 1]
             if y != 0:
-                first, count = pairs_x[x]
-                return (low if y < 0 else high).at[:, pl.ds(first, count)]
-            first, count = slices_x[x]
-            return own.at[:, pl.ds(first, count)]
+                return (s.hw_low if y < 0 else s.hw_high).at[:, pl.ds(*pairs_x[x])]
+            return s.hw_own.at[:, pl.ds(*slices_x[x])]
 
         def target(k):
             x, y, z = AROUND[k]
             if z != 0:
-                return get("zr").at[flat_zr.index((x, y, z))]
+                return s.hw_zr.at[flat_zr.index((x, y, z))]
             if y != 0:
-                return get("yr").at[flat_yr.index((x, y)), :, pl.ds(0, pairs_x[x][1])]
-            return get("xr").at[0 if x > 0 else 1, :, pl.ds(0, slices_x[x][1])]
-
-        return copies(AROUND, source, target, get("ss"), get("rs"))
-
-    def assemble(arrays, key):
-        get = lambda name: getattr(s, f"{key}_{name}")
-        own, xr, yr, zr, ext = get("own"), get("xr"), get("yr"), get("zr"), get("ext")
-        first8 = (lane8 & 15) < 8
-        side_high, side_low = (lane16 >= 64) & (lane16 < 72), lane16 >= 120
-
-        def zed(a, x, y):
-            above = zr[flat_zr.index((x, y, -1)), a]
-            below = zr[flat_zr.index((x, y, 1)), a]
-            return jnp.where(first8, above, below)
-
-        for a in range(arrays):
-            combs = {}
-            for x in (1, -1, 0):
-                outer = jnp.where(upper_half, zed(a, x, -1), zed(a, x, 1))
-                combs[x] = jnp.concatenate([zed(a, x, 0), outer], axis=0)
-            for k in range(17):
-                x = k - 4
-                if x < 0:
-                    d, layer, place = 1, x + 4, x + 8
-                elif x < 8:
-                    d, layer, place = 0, x, x
-                else:
-                    d, layer, place = -1, x - 8, x - 8
-                inner = own[a, layer] if d == 0 else xr[0 if d > 0 else 1, a, layer]
-                above = yr[flat_yr.index((d, -1)), a, layer // 2]
-                below = yr[flat_yr.index((d, 1)), a, layer // 2]
-                if layer % 2 == 0:
-                    below = turn(below, 4, 0)
-                else:
-                    above = turn(above, 4, 0)
-                outer = jnp.where(upper_half, above, below)
-                whole = jnp.concatenate([inner, outer], axis=0)
-                comb = combs[d]
-                whole = jnp.where(side_high, turn(comb, 64 - 16 * place), whole)
-                whole = jnp.where(side_low, turn(comb, 112 - 16 * place), whole)
-                ext[a, pl.ds(16 * k, 16)] = whole
+                return s.hw_yr.at[flat_yr.index((x, y)), :, pl.ds(0, pairs_x[x][1])]
+            return s.hw_xr.at[0 if x > 0 else 1]
+
+        return copies(AROUND, source, target, s.hw_ss, s.hw_rs)
+
+    def assemble(a, k):
+        x = k - 4
+        if x < 0:
+            d, layer, first = 1, x + 8, 5
+        elif x < 8:
+            d, layer, first = 0, x, 0
+        else:
+            d, layer, first = -1, x - 8, 0
+        place = 3 * (8 * a + layer)
+        inner = s.hw_own[a, layer] if d == 0 else s.hw_xr[0 if d > 0 else 1, a, layer - first]
+        pair = layer // 2 - pairs_x[d][0]
+        above = s.hw_yr[flat_yr.index((d, -1)), a, pair]
+        below = s.hw_yr[flat_yr.index((d, 1)), a, pair]
+        if layer % 2 == 0:
+            below = turn(below, 4, 0)
+        else:
+            above = turn(above, 4, 0)
+        outer = jnp.where(upper_half, above, below)
+        whole = jnp.concatenate([inner, outer], axis=0)
+
+        def side(z):
+            zed = lambda y: s.hw_zr[flat_zr.index((d, y, z))]
+            outer = jnp.where(upper_half, zed(-1), zed(1))
+            return jnp.concatenate([zed(0), outer], axis=0)
+
+        whole = jnp.where((lane16 >= 64) & (lane16 < 72), turn(side(-1), 64 - place), whole)
+        return jnp.where(lane16 >= 120, turn(side(1), 125 - place), whole)
 
     def ext1(k):
         return pl.ds(16 * k, 16)
@@ -411,29 +393,57 @@
     def pad1(k):
         return pl.ds(16 * k + 16, 16)
 
-    def coefficients1():
+    def coefficients1(first, last):
         keep_y = jnp.where(row16 == 0, low_y, 1.0)
         keep_z = jnp.where(lane16 == 0, low_z, 1.0)
+        last_y = jnp.where(row16 == 7, top_y, 1.0)
         last_z = jnp.where(lane16 == 63, top_z, 1.0)
-        for k in range(16):
+        for k in range(first, last + 1):
             own = ext1(k)
-            a_xl, a_yl, a_zl = s.hf_ext[0, own], s.hf_ext[1, own], s.hf_ext[2, own]
-            a_xu = s.hf_ext[0, ext1(k + 1)]
+            a_xl, a_yl, a_zl = s.ext1[0, own], s.ext1[1, own], s.ext1[2, own]
+            a_xu = s.ext1[0, ext1(k + 1)]
             if k == 11:
                 a_xu = a_xu * top_x
-            a_yu = s.hf_ext[3, own]
+            a_yu = turn(a_yl, -1, 0) * last_y
             a_zu = turn(a_zl, -1) * last_z
             total = (a_xl + a_yl + a_zl) + (a_xu + a_yu + a_zu)
             scale = RELAX / total
             s.kw1[own] = scale * 4.0
-            if 1 <= k <= 14:
-                s.d151[own] = (1.5 * 0.25) * total
-                s.cxl1[own] = scale * a_xl * (low_x if k == 4 else 1.0)
-                s.cxu1[own] = scale * a_xu
-                s.cyl1[own] = scale * a_yl * keep_y
-                s.cyu1[own] = scale * a_yu
-                s.czl1[own] = scale * a_zl * keep_z
-                s.czu1[own] = scale * a_zu
+            s.d151[own] = (1.5 * 0.25) * total
+            s.cxl1[own] = scale * a_xl * (low_x if k == 4 else 1.0)
+            s.cxu1[own] = scale * a_xu
+            s.cyl1[own] = scale * a_yl * keep_y
+            s.cyu1[own] = scale * a_yu
+            s.czl1[own] = scale * a_zl * keep_z
+            s.czu1[own] = scale * a_zu
+
+    def send_faces1(ref, key):
+        snd, rcv = getattr(s, key + "_snd"), getattr(s, key + "_rcv")
+        inner = lambda i: ref[pl.ds(16 * (i + 5), 8)]
+        snd[0] = inner(7)
+        snd[1] = inner(0)
+        snd[2] = ref[pl.ds(16 * 5 + 7, 8, stride=16)]
+        snd[3] = ref[pl.ds(16 * 5, 8, stride=16)]
+        snd[4] = pack(inner, 8, 8, 63)
+        snd[5] = pack(inner, 8, 8, 0)
+        return copies(
+            FACES,
+            lambda k: snd.at[k],
+            lambda k: rcv.at[k],
+            getattr(s, key + "_ss"),
+            getattr(s, key + "_rs"),
+        )
+
+    def fill1(ref, halo):
+        low, high = halo[4], halo[5]
+        for i in range(8):
+            own = pl.ds(16 * (i + 5), 8)
+            v = jnp.where(lane8 == 64, turn(high, 64 - i), ref[own])
+            ref[own] = jnp.where(lane8 == 127, turn(low, 127 - i), v)
+        ref[pl.ds(16 * 4, 8)] = halo[0]
+        ref[pl.ds(16 * 13, 8)] = halo[1]
+        ref[pl.ds(16 * 5 + 15, 8, stride=16)] = halo[2]
+        ref[pl.ds(16 * 5 + 8, 8, stride=16)] = halo[3]
 
     def stencil1(first, last, ref, emit):
         for k in range(first, last + 1):
@@ -477,6 +487,8 @@
 
     for load in loads[:3]:
         load.wait()
+    round_a0 = send_upper(s.fx, s.fy, s.fz, "a0")
+
     for i in range(8):
         own = pl.ds(8 * i, 8)
         here = lambda ref, shift: ref[pl.ds(32 * i + shift, 8, stride=2)]
@@ -484,6 +496,12 @@
         s.fy1[own] = take(pair_z(here(s.fy, 0) + here(s.fy, 16)), even8) * 0.25
         total = (here(s.fz, 0) + here(s.fz, 1)) + (here(s.fz, 16) + here(s.fz, 17))
         s.fz1[own] = take(total, even8) * 0.25
+    s.a1_snd[0] = s.fx1[pl.ds(0, 8)]
+    s.a1_snd[1] = s.fy1[pl.ds(0, 8, stride=8)]
+    s.a1_snd[2] = pack(lambda i: s.fz1[pl.ds(8 * i, 8)], 8, 8, 0)
+    round_a1 = copies(
+        DOWN, lambda k: s.a1_snd.at[k], lambda k: s.a1_rcv.at[k], s.a1_ss, s.a1_rs
+    )
     for i in range(4):
         own = pl.ds(4 * i, 4)
         here = lambda ref, shift: ref[pl.ds(16 * i + shift, 4, stride=2)]
@@ -508,14 +526,11 @@
             ref[pl.ds(8 * k, 8)] = jnp.zeros((8, 128), F32)
             ref[pl.ds(144 + 8 * k, 8)] = jnp.zeros((8, 128), F32)
     s.p2[...] = jnp.zeros_like(s.p2)
-    s.a1_snd[...] = s.fy1[pl.ds(0, 8, stride=8)]
-
-    pl.semaphore_wait(barrier, len(friends))
-    round_a0 = send_upper(s.fx, s.fy, s.fz, "a0")
-    round_a1 = copies([DOWN[1]], lambda k: s.a1_snd, lambda k: s.a1_rcv, s.a1_ss, s.a1_rs)
-    round_zf = copies(
-        RING_Z, lambda k: s.zf_snd, lambda k: s.zf_rcv.at[k], s.zf_ss, s.zf_rs
-    )
+    s.ext1[...] = jnp.ones_like(s.ext1)
+    for k in (0, 1, 2, 3, 12, 13, 14, 15):
+        s.va1[pad1(k)] = jnp.zeros((16, 128), F32)
+        s.vb1[pad1(k)] = jnp.zeros((16, 128), F32)
+
     loads[3].wait()
     finish(round_a0)
     coefficients(0, s.fx, s.fy, s.fz, "a0")
@@ -527,36 +542,50 @@
     round_b = send_faces(B0, s.va0, "b")
     finish(round_a1)
     for i in range(8):
-        s.lyp1[pl.ds(16 * i, 8)] = s.fy1[pl.ds(8 * i, 8)]
-    s.lyp1[pl.ds(8, 8, stride=16)] = s.a1_rcv[...] * top_y
-    for i in range(8):
-        own = pl.ds(8 * i, 8)
-        s.hf_own[0, i] = s.fx1[own]
-        s.hf_own[1, i] = s.fy1[own]
-        s.hf_own[2, i] = s.fz1[own]
-        s.hf_own[3, i] = s.lyp1[pl.ds(16 * i + 1, 8)]
+        own, here = pl.ds(8 * i, 8), pl.ds(16 * (i + 4), 8)
+        s.ext1[0, here] = s.fx1[own]
+        s.ext1[1, here] = s.fy1[own]
+        upper = turn(s.a1_rcv[2], 64 - i)
+        s.ext1[2, here] = jnp.where(lane8 == 64, upper, s.fz1[own])
+        s.hw_own[0, i] = s.fx1[own]
+        s.hw_own[1, i] = s.fy1[own]
+        s.hw_own[2, i] = s.fz1[own]
+    s.ext1[0, pl.ds(16 * 12, 8)] = s.a1_rcv[0]
+    s.ext1[1, pl.ds(16 * 4 + 8, 8, stride=16)] = s.a1_rcv[1]
+    coefficients1(4, 11)
     finish(round_b)
     fill(B0, s.va0, s.b_rcv)
     smooth(0, s.va0, s.vb0, s.b_rcv[4], s.b_rcv[5])
     round_c = send_faces(B0, s.vb0, "c")
-    round_hf = send_around(4, "hf")
+    finish(round_c)
+    fill(B0, s.vb0, s.c_rcv)
+    residual(0, s.vb0, s.c_rcv[4], s.c_rcv[5])
+
+    for i in range(8):
+        here = lambda shift: s.r0[pl.ds(32 * i + shift, 8, stride=2)]
+        total = (here(0) + here(1)) + (here(16) + here(17))
+        forcing = take(pair_z(total), even8) * 0.125
+        s.hw_own[3, i] = forcing
+        start = s.kw1[pl.ds(16 * (i + 4), 8)] * forcing
+        s.g1[pl.ds(16 * (i + 4), 8)] = start
+        s.g1[pl.ds(16 * (i + 4) + 8, 8)] = jnp.zeros((8, 128), F32)
+        s.va1[pl.ds(16 * (i + 5), 8)] = start
+        s.va1[pl.ds(16 * (i + 5) + 8, 8)] = jnp.zeros((8, 128), F32)
+    round_d = send_faces1(s.va1, "d")
+    round_zf = copies(
+        RING_Z, lambda k: s.zf_snd, lambda k: s.zf_rcv.at[k], s.zf_ss, s.zf_rs
+    )
+    finish(round_d)
+    fill1(s.va1, s.d_rcv)
+    smooth1(4, 11, s.va1, s.vb1)
+    for i in range(8):
+        s.hw_own[4, i] = s.vb1[pl.ds(16 * (i + 5), 8)]
+    round_e = send_faces1(s.vb1, "e")
     finish(round_zf)
     merge_z(3, s.zf_snd, s.zf_rcv, s.xf_snd)
     round_xf = copies(
         LINE, lambda k: s.xf_snd, lambda k: s.xf_rcv.at[k], s.xf_ss, s.xf_rs
     )
-    finish(round_c)
-    fill(B0, s.vb0, s.c_rcv)
-    residual(0, s.vb0, s.c_rcv[4], s.c_rcv[5])
-
-    for i in range(8):
-        here = lambda shift: s.r0[pl.ds(32 * i + shift, 8, stride=2)]
-        total = (here(0) + here(1)) + (here(16) + here(17))
-        s.hr_own[0, i] = take(pair_z(total), even8) * 0.125
-    round_hr = send_around(1, "hr")
-    finish(round_hf)
-    assemble(4, "hf")
-    coefficients1()
 
 
     def block2(p, x):
@@ -604,19 +633,11 @@
                     ref[p, x + 2, pl.ds(8, 8)] = jnp.where(upper_half, above, rest)
 
     faces2 = (s.lx2, s.ly2, s.lz2)
-    finish(round_xf)
-    spread(3, LINE, s.xf_snd, s.xf_rcv, faces2)
-    round_nf = send_sides(faces2, "nf")
     global_y = row16 + 4 * gy - 4
     not_low, not_top = global_y != 0, global_y != 4 * GY - 1
 
-    finish(round_hr)
-    assemble(1, "hr")
-    for k in range(16):
-        start = s.kw1[ext1(k)] * s.hr_ext[0, ext1(k)]
-        s.g1[ext1(k)] = start
-        s.va1[pad1(k)] = start
-    smooth1(1, 14, s.va1, s.vb1)
+    finish(round_e)
+    fill1(s.vb1, s.e_rcv)
 
     def emit_r1(k, v, total):
         r = s.d151[ext1(k)] * (total - RELAX * v)
@@ -632,8 +653,9 @@
         RING_Z, lambda k: s.zr_snd, lambda k: s.zr_rcv.at[k], s.zr_ss, s.zr_rs
     )
 
-    finish(round_nf)
-    take_sides(faces2, "nf", 1.0)
+    finish(round_xf)
+    spread(3, LINE, s.xf_snd, s.xf_rcv, faces2)
+    round_nf = send_sides(faces2, "nf")
 
     for a, ref in enumerate((s.lx2, s.ly2, s.lz2)):
         for i in range(8):
@@ -658,7 +680,33 @@
         s.yf_ss,
         s.yf_rs,
     )
-
+    round_hw = send_around()
+
+    def stencil2(ref, emit):
+        for p in range(2):
+            for x in range(16):
+                j, other = block2(p, x), block2(1 - p, x)
+                v, w = ref[j], ref[other]
+                t_x = s.cxl2[j] * ref[block2(p, x - 1)] + s.cxu2[j] * ref[block2(p, x + 1)]
+                t_y = s.cyl2[j] * turn(v, 1, 0) + s.cyu2[j] * turn(v, -1, 0)
+                down, up = (turn(w, 1), w) if p == 0 else (w, turn(w, -1))
+                t_z = s.czl2[j] * down + s.czu2[j] * up
+                emit(j, v, s.g2[j] + (t_x + t_y + t_z))
+
+    def smooth2(source, target):
+        def emit(j, v, total):
+            target[j] = v * THIRD + total
+
+        stencil2(source, emit)
+
+    finish(round_zr)
+    merge_z(1, s.zr_snd, s.zr_rcv, s.xr_snd)
+    round_xr = copies(
+        PLANE, lambda k: s.xr_snd, lambda k: s.xr_rcv.at[k], s.xr_ss, s.xr_rs
+    )
+
+    finish(round_nf)
+    take_sides(faces2, "nf", 1.0)
     for p in range(2):
         for x in range(16):
             j = block2(p, x)
@@ -679,29 +727,6 @@
             s.cyu2[j] = scale * a_yu
             s.czl2[j] = scale * a_zl if p == 1 else jnp.where(lane16 == 0, 0.0, scale * a_zl)
             s.czu2[j] = scale * a_zu
-
-    def stencil2(ref, emit):
-        for p in range(2):
-            for x in range(16):
-                j, other = block2(p, x), block2(1 - p, x)
-                v, w = ref[j], ref[other]
-                t_x = s.cxl2[j] * ref[block2(p, x - 1)] + s.cxu2[j] * ref[block2(p, x + 1)]
-                t_y = s.cyl2[j] * turn(v, 1, 0) + s.cyu2[j] * turn(v, -1, 0)
-                down, up = (turn(w, 1), w) if p == 0 else (w, turn(w, -1))
-                t_z = s.czl2[j] * down + s.czu2[j] * up
-                emit(j, v, s.g2[j] + (t_x + t_y + t_z))
-
-    def smooth2(source, target):
-        def emit(j, v, total):
-            target[j] = v * THIRD + total
-
-        stencil2(source, emit)
-
-    finish(round_zr)
-    merge_z(1, s.zr_snd, s.zr_rcv, s.xr_snd)
-    round_xr = copies(
-        PLANE, lambda k: s.xr_snd, lambda k: s.xr_rcv.at[k], s.xr_ss, s.xr_rs
-    )
 
     finish(round_yf)
     zero8 = jnp.zeros((8, 128), F32)
@@ -813,6 +838,15 @@
         RING_Y, lambda k: s.f3.at[mine], lambda k: s.f3.at[mine], s.yr_ss, s.yr_rs
     )
     round_nv = send_sides((s.vb2,), "nv")
+
+    finish(round_hw)
+    for k in range(1, 15):
+        for a in range(4):
+            s.ext1[a, ext1(k)] = assemble(a, k)
+        s.vb1[pad1(k)] = assemble(4, k)
+    coefficients1(2, 13)
+    for k in range(2, 14):
+        s.g1[ext1(k)] = s.kw1[ext1(k)] * s.ext1[3, ext1(k)]
     finish(round_yr)
 
     def at3(y):
@@ -958,7 +992,7 @@
         out_specs=pl.BlockSpec(memory_space=pltpu.VMEM),
         scratch_shapes=list(SCRATCH.values()),
         compiler_params=pltpu.CompilerParams(
-            collective_id=0, has_side_effects=True, vmem_limit_bytes=48 * 1024 * 1024
+            collective_id=0, has_side_effects=True, vmem_limit_bytes=64 * 1024 * 1024
         ),
         name="vcycle",
     )(*flat)

time: 61.3 us -> 61.1 us (level)
  Pallas kernels: 56.6 us -> 59.4 us
  local copies, waits for them, and re-layouts: 4.27 us -> 1.57 us
    pallas_call x1, Pallas kernels: 56.6 us -> 59.4 us  [shards(): pl.pallas_call(cycle, out_shape=jax.ShapeDtypeStruct((256, 128), F32), in...]
    unnamed x9 -> x1, local copies, waits for them, and re-layouts: 4.27 us -> 1.57 us
where the time goes in v2:
time: 61.1 us; the launch traced here: 61 us
  Pallas kernels  59.4 us (97%)
  local copies, waits for them, and re-layouts  1.57 us (3%)
    pallas_call x1, Pallas kernels, shards(): pl.pallas_call(cycle, out_shape=jax.ShapeDtypeStruct((256, 128), F32), in...  59.4 us
    unnamed x1, local copies, waits for them, and re-layouts  1.57 us

profile of v2, /device:TPU:1, one launch (start us, length us, event | category | flops | bytes accessed | tf_op | source)
XLA Modules:
  0.0 61.0 jit_solution(2627499451198231300)
XLA Ops:
  0.0 59.4 %vcycle.1 = f32[256,128]{1,0:T(8,128)} custom-call(f32[256,128]{1,0:T(8,128)} %bitcast.6, f32[256,128]{1,0:T(8,128)} %bitcast.7, f32[256,128]{1,0:T(8,128)} %bitcast.8, f32[256,128]{1,0:T(8,128)} %bitcast.9), custom_call_target="tpu_custom_call" | custom-call | tf_op jit(solution)/shard_map/vcycle/pallas_call | solution.py:988
  59.4 1.6 %copy.6 = f32[16,16,128]{2,1,0:T(8,128)} copy(f32[16,16,128]{2,1,0:T(8,128)} %bitcast.5) | data formatting | bytes 262144

commit v3 on v2

--- a/solution.py
+++ b/solution.py
@@ -92,11 +92,12 @@
     vmem(key, 19 * 16, 128)
 vmem("ext1", 4, 17 * 16, 128)
 vmem("hw_own", 5, 8, 8, 128)
-vmem("hw_low", 5, 4, 8, 128)
-vmem("hw_high", 5, 4, 8, 128)
+vmem("hw_pack", 3, 8, 8, 128)
+vmem("hw_low", 3, 4, 8, 128)
+vmem("hw_high", 3, 4, 8, 128)
 vmem("hw_zed", 2, 8, 128)
-vmem("hw_xr", 2, 5, 3, 8, 128)
-vmem("hw_yr", 6, 5, 4, 8, 128)
+vmem("hw_xr", 2, 3, 3, 8, 128)
+vmem("hw_yr", 6, 3, 4, 8, 128)
 vmem("hw_zr", 18, 8, 128)
 dma("hw_ss", 26)
 dma("hw_rs", 26)
@@ -108,25 +109,24 @@
     dma(f"{key}_ss", count)
     dma(f"{key}_rs", count)
 vmem("t16", 3, 16, 128)
-for key, arrays in (("zf", 3), ("zr", 1)):
-    vmem(f"{key}_snd", 16, 128)
-    vmem(f"{key}_rcv", 7, 16, 128)
-    dma(f"{key}_ss", 7)
-    dma(f"{key}_rs", 7)
-for key, arrays in (("xf", 3), ("xr", 1)):
-    vmem(f"{key}_snd", arrays * 2, 16, 128)
-    vmem(f"{key}_rcv", 11, arrays * 2, 16, 128)
-    dma(f"{key}_ss", 11)
-    dma(f"{key}_rs", 11)
+vmem("zf_snd", 4, 3, 16, 128)
+vmem("zf_rcv", 7, 4, 3, 16, 128)
+vmem("zr_snd", 16, 128)
+vmem("zr_rcv", 7, 16, 128)
+vmem("xr_snd", 2, 16, 128)
+vmem("xr_rcv", 11, 2, 16, 128)
+vmem("m2", 6, 16, 128)
+for key, count in (("zf", 7), ("zr", 7), ("xr", 11), ("xf", 3), ("nf", 2)):
+    dma(f"{key}_ss", count)
+    dma(f"{key}_rs", count)
 for key in ("f2", "lx2", "ly2", "lz2", "va2", "vb2"):
     vmem(key, 2, 20, 16, 128)
 for key in ("cxl2", "cxu2", "cyl2", "cyu2", "czl2", "czu2", "g2", "d152", "kw2"):
     vmem(key, 2, 20, 16, 128)
-for key, arrays in (("nf", 3), ("nv", 1)):
-    vmem(f"{key}_snd", arrays, 2, 8, 8, 128)
-    vmem(f"{key}_rcv", 2, arrays, 2, 8, 8, 128)
-    dma(f"{key}_ss", 2)
-    dma(f"{key}_rs", 2)
+vmem("nv_snd", 1, 2, 8, 8, 128)
+vmem("nv_rcv", 2, 1, 2, 8, 8, 128)
+dma("nv_ss", 2)
+dma("nv_rs", 2)
 vmem("s2", 128, 128)
 vmem("p2", 256, 128)
 vmem("face3", 3, 128, 128)
@@ -329,10 +329,6 @@
         zeds = [jnp.zeros((8, 128), F32)] * 2
         group = lane8 // 3
         for a in range(5):
-            for i in range(4):
-                even, odd = s.hw_own[a, 2 * i], s.hw_own[a, 2 * i + 1]
-                s.hw_low[a, i] = jnp.where(upper_half, even, turn(odd, 4, 0))
-                s.hw_high[a, i] = jnp.where(upper_half, turn(even, 4, 0), odd)
             for x in range(8):
                 v, place = s.hw_own[a, x], 8 * a + x
                 zeds = [
@@ -340,6 +336,18 @@
                     for zed, first in zip(zeds, (61, 0))
                 ]
         s.hw_zed[0], s.hw_zed[1] = zeds
+        for t in range(3):
+            tiles = []
+            for x in range(8):
+                v = s.hw_own[2 * t, x]
+                if t < 2:
+                    v = jnp.where(lane8 < 64, v, turn(s.hw_own[2 * t + 1, x], 64))
+                s.hw_pack[t, x] = v
+                tiles.append(v)
+            for i in range(4):
+                even, odd = tiles[2 * i], tiles[2 * i + 1]
+                s.hw_low[t, i] = jnp.where(upper_half, even, turn(odd, 4, 0))
+                s.hw_high[t, i] = jnp.where(upper_half, turn(even, 4, 0), odd)
 
         def source(k):
             x, y, z = AROUND[k]
@@ -347,7 +355,7 @@
                 return s.hw_zed.at[0 if z > 0 else 1]
             if y != 0:
                 return (s.hw_low if y < 0 else s.hw_high).at[:, pl.ds(*pairs_x[x])]
-            return s.hw_own.at[:, pl.ds(*slices_x[x])]
+            return s.hw_pack.at[:, pl.ds(*slices_x[x])]
 
         def target(k):
             x, y, z = AROUND[k]
@@ -368,15 +376,19 @@
         else:
             d, layer, first = -1, x - 8, 0
         place = 3 * (8 * a + layer)
-        inner = s.hw_own[a, layer] if d == 0 else s.hw_xr[0 if d > 0 else 1, a, layer - first]
+        t = a // 2
+        inner = s.hw_own[a, layer] if d == 0 else s.hw_xr[0 if d > 0 else 1, t, layer - first]
         pair = layer // 2 - pairs_x[d][0]
-        above = s.hw_yr[flat_yr.index((d, -1)), a, pair]
-        below = s.hw_yr[flat_yr.index((d, 1)), a, pair]
+        above = s.hw_yr[flat_yr.index((d, -1)), t, pair]
+        below = s.hw_yr[flat_yr.index((d, 1)), t, pair]
         if layer % 2 == 0:
             below = turn(below, 4, 0)
         else:
             above = turn(above, 4, 0)
         outer = jnp.where(upper_half, above, below)
+        if a % 2 == 1:
+            outer = turn(outer, 64)
+            inner = inner if d == 0 else turn(inner, 64)
         whole = jnp.concatenate([inner, outer], axis=0)
 
         def side(z):
@@ -476,9 +488,9 @@
                 packed = jnp.where(group == ((gz + 2 * a + p) & 7), moved, packed)
         snd[...] = packed
 
-    def merge_z(arrays, snd, rcv, target):
+    def merge_z(arrays, own, others, target):
         group = lane16 >> 4
-        parts = [(0, snd[...])] + [(RING_Z[k][2], rcv[k]) for k in range(7)]
+        parts = [(0, own)] + [(RING_Z[k][2], others(k)) for k in range(7)]
         for q in range(2 * arrays):
             merged = jnp.zeros((16, 128), F32)
             for distance, part in parts:
@@ -511,11 +523,17 @@
         s.t16[2, own] = total * 0.25
     s.t16[0] = pair_z(s.t16[0]) * 0.25
     s.t16[1] = pair_z(s.t16[1]) * 0.25
-    stage_z(3, s.zf_snd)
+    stage_z(3, s.zf_snd.at[0, 0])
+    round_nf = copies(
+        SIDES, lambda k: s.zf_snd.at[0, 0], lambda k: s.zf_snd.at[0, k + 1], s.nf_ss, s.nf_rs
+    )
     for ref in (s.va1, s.vb1):
         for k in (-1, 17):
             ref[pad1(k)] = jnp.zeros((16, 128), F32)
     for p in range(2):
+        for x in range(16):
+            for ref in (s.lx2, s.ly2, s.lz2):
+                ref[p, x + 2, pl.ds(8, 8)] = jnp.ones((8, 128), F32)
         for x in (0, 1, 18, 19):
             for ref in (s.va2, s.vb2):
                 ref[p, x] = jnp.zeros((16, 128), F32)
@@ -554,6 +572,10 @@
     s.ext1[1, pl.ds(16 * 4 + 8, 8, stride=16)] = s.a1_rcv[1]
     coefficients1(4, 11)
     finish(round_b)
+    finish(round_nf)
+    round_xf = copies(
+        LINE, lambda k: s.zf_snd.at[0], lambda k: s.zf_snd.at[k + 1], s.xf_ss, s.xf_rs
+    )
     fill(B0, s.va0, s.b_rcv)
     smooth(0, s.va0, s.vb0, s.b_rcv[4], s.b_rcv[5])
     round_c = send_faces(B0, s.vb0, "c")
@@ -572,6 +594,7 @@
         s.va1[pl.ds(16 * (i + 5), 8)] = start
         s.va1[pl.ds(16 * (i + 5) + 8, 8)] = jnp.zeros((8, 128), F32)
     round_d = send_faces1(s.va1, "d")
+    finish(round_xf)
     round_zf = copies(
         RING_Z, lambda k: s.zf_snd, lambda k: s.zf_rcv.at[k], s.zf_ss, s.zf_rs
     )
@@ -581,11 +604,6 @@
     for i in range(8):
         s.hw_own[4, i] = s.vb1[pl.ds(16 * (i + 5), 8)]
     round_e = send_faces1(s.vb1, "e")
-    finish(round_zf)
-    merge_z(3, s.zf_snd, s.zf_rcv, s.xf_snd)
-    round_xf = copies(
-        LINE, lambda k: s.xf_snd, lambda k: s.xf_rcv.at[k], s.xf_ss, s.xf_rs
-    )
 
 
     def block2(p, x):
@@ -653,10 +671,44 @@
         RING_Z, lambda k: s.zr_snd, lambda k: s.zr_rcv.at[k], s.zr_ss, s.zr_rs
     )
 
-    finish(round_xf)
-    spread(3, LINE, s.xf_snd, s.xf_rcv, faces2)
-    round_nf = send_sides(faces2, "nf")
-
+
+    mine = pl.ds(pl.multiple_of(16 * gy, 16), 16)
+    round_hw = send_around()
+
+    def stencil2(ref, emit):
+        for p in range(2):
+            for x in range(16):
+                j, other = block2(p, x), block2(1 - p, x)
+                v, w = ref[j], ref[other]
+                t_x = s.cxl2[j] * ref[block2(p, x - 1)] + s.cxu2[j] * ref[block2(p, x + 1)]
+                t_y = s.cyl2[j] * turn(v, 1, 0) + s.cyu2[j] * turn(v, -1, 0)
+                down, up = (turn(w, 1), w) if p == 0 else (w, turn(w, -1))
+                t_z = s.czl2[j] * down + s.czu2[j] * up
+                emit(j, v, s.g2[j] + (t_x + t_y + t_z))
+
+    def smooth2(source, target):
+        def emit(j, v, total):
+            target[j] = v * THIRD + total
+
+        stencil2(source, emit)
+
+    finish(round_zr)
+    merge_z(1, s.zr_snd[...], lambda k: s.zr_rcv[k], s.xr_snd)
+    round_xr = copies(
+        PLANE, lambda k: s.xr_snd, lambda k: s.xr_rcv.at[k], s.xr_ss, s.xr_rs
+    )
+
+    finish(round_zf)
+    for line in range(4):
+        first = 4 * ((gx - ((0, 0, 0), *LINE)[line][0]) & 3)
+        for side in range(3):
+            place = pl.ds((4, 0, 8)[side], 4)
+            merge_z(3, s.zf_snd[line, side], lambda k: s.zf_rcv[k, line, side], s.m2)
+            for a in range(3):
+                for p in range(2):
+                    for x in range(4):
+                        piece = s.m2[2 * a + p, pl.ds(4 * x, 4)]
+                        faces2[a][p, x + 2 + first, place] = piece
     for a, ref in enumerate((s.lx2, s.ly2, s.lz2)):
         for i in range(8):
             total = ref[block2(0, 2 * i)]
@@ -672,7 +724,6 @@
             if a != 1:
                 total = total + s.s2[pl.ds(5 + 2 * j, 8, stride=16)]
             s.face3[a, pl.ds(pl.multiple_of(16 * gy + 8 * j, 8), 8)] = total * 0.25
-    mine = pl.ds(pl.multiple_of(16 * gy, 16), 16)
     round_yf = copies(
         RING_Y,
         lambda k: s.face3.at[:, mine],
@@ -680,33 +731,6 @@
         s.yf_ss,
         s.yf_rs,
     )
-    round_hw = send_around()
-
-    def stencil2(ref, emit):
-        for p in range(2):
-            for x in range(16):
-                j, other = block2(p, x), block2(1 - p, x)
-                v, w = ref[j], ref[other]
-                t_x = s.cxl2[j] * ref[block2(p, x - 1)] + s.cxu2[j] * ref[block2(p, x + 1)]
-                t_y = s.cyl2[j] * turn(v, 1, 0) + s.cyu2[j] * turn(v, -1, 0)
-                down, up = (turn(w, 1), w) if p == 0 else (w, turn(w, -1))
-                t_z = s.czl2[j] * down + s.czu2[j] * up
-                emit(j, v, s.g2[j] + (t_x + t_y + t_z))
-
-    def smooth2(source, target):
-        def emit(j, v, total):
-            target[j] = v * THIRD + total
-
-        stencil2(source, emit)
-
-    finish(round_zr)
-    merge_z(1, s.zr_snd, s.zr_rcv, s.xr_snd)
-    round_xr = copies(
-        PLANE, lambda k: s.xr_snd, lambda k: s.xr_rcv.at[k], s.xr_ss, s.xr_rs
-    )
-
-    finish(round_nf)
-    take_sides(faces2, "nf", 1.0)
     for p in range(2):
         for x in range(16):
             j = block2(p, x)
@@ -727,6 +751,33 @@
             s.cyu2[j] = scale * a_yu
             s.czl2[j] = scale * a_zl if p == 1 else jnp.where(lane16 == 0, 0.0, scale * a_zl)
             s.czu2[j] = scale * a_zu
+
+    finish(round_xr)
+    spread(1, PLANE, s.xr_snd, s.xr_rcv, (s.f2,))
+    for p in range(2):
+        for x in range(16):
+            j = block2(p, x)
+            start = s.kw2[j] * s.f2[j]
+            s.g2[j] = start
+            s.va2[j] = start
+    smooth2(s.va2, s.vb2)
+
+    def emit_r2(j, v, total):
+        s.f2[j] = s.d152[j] * (total - RELAX * v)
+
+    stencil2(s.vb2, emit_r2)
+    for i in range(8):
+        total = (s.f2[block2(0, 2 * i)] + s.f2[block2(1, 2 * i)]) + (
+            s.f2[block2(0, 2 * i + 1)] + s.f2[block2(1, 2 * i + 1)]
+        )
+        s.s2[pl.ds(16 * i, 16)] = total
+    for j in range(2):
+        total = s.s2[pl.ds(4 + 2 * j, 8, stride=16)] + s.s2[pl.ds(5 + 2 * j, 8, stride=16)]
+        s.f3[pl.ds(pl.multiple_of(16 * gy + 8 * j, 8), 8)] = total * 0.125
+    round_yr = copies(
+        RING_Y, lambda k: s.f3.at[mine], lambda k: s.f3.at[mine], s.yr_ss, s.yr_rs
+    )
+    round_nv = send_sides((s.vb2,), "nv")
 
     finish(round_yf)
     zero8 = jnp.zeros((8, 128), F32)
@@ -812,33 +863,6 @@
     s.czl5[...] = jnp.where(lane8 < 4, 0.0, scale * a_zl)
     s.czu5[...] = scale * a_zu
 
-    finish(round_xr)
-    spread(1, PLANE, s.xr_snd, s.xr_rcv, (s.f2,))
-    for p in range(2):
-        for x in range(16):
-            j = block2(p, x)
-            start = s.kw2[j] * s.f2[j]
-            s.g2[j] = start
-            s.va2[j] = start
-    smooth2(s.va2, s.vb2)
-
-    def emit_r2(j, v, total):
-        s.f2[j] = s.d152[j] * (total - RELAX * v)
-
-    stencil2(s.vb2, emit_r2)
-    for i in range(8):
-        total = (s.f2[block2(0, 2 * i)] + s.f2[block2(1, 2 * i)]) + (
-            s.f2[block2(0, 2 * i + 1)] + s.f2[block2(1, 2 * i + 1)]
-        )
-        s.s2[pl.ds(16 * i, 16)] = total
-    for j in range(2):
-        total = s.s2[pl.ds(4 + 2 * j, 8, stride=16)] + s.s2[pl.ds(5 + 2 * j, 8, stride=16)]
-        s.f3[pl.ds(pl.multiple_of(16 * gy + 8 * j, 8), 8)] = total * 0.125
-    round_yr = copies(
-        RING_Y, lambda k: s.f3.at[mine], lambda k: s.f3.at[mine], s.yr_ss, s.yr_rs
-    )
-    round_nv = send_sides((s.vb2,), "nv")
-
     finish(round_hw)
     for k in range(1, 15):
         for a in range(4):

time: 61.1 us -> 55.6 us (0.910)
  Pallas kernels: 59.4 us -> 54 us
    pallas_call x1, Pallas kernels: 59.4 us -> 54 us  [shards(): pl.pallas_call(cycle, out_shape=jax.ShapeDtypeStruct((256, 128), F32), in...]
where the time goes in v3:
time: 55.6 us; the launch traced here: 55.5 us
  Pallas kernels  54 us (97%)
  local copies, waits for them, and re-layouts  1.57 us (3%)
    pallas_call x1, Pallas kernels, shards(): pl.pallas_call(cycle, out_shape=jax.ShapeDtypeStruct((256, 128), F32), in...  54 us
    unnamed x1, local copies, waits for them, and re-layouts  1.57 us

profile of v3, /device:TPU:1, one launch (start us, length us, event | category | flops | bytes accessed | tf_op | source)
XLA Modules:
  0.0 55.5 jit_solution(12581100053581083168)
XLA Ops:
  0.0 54.0 %vcycle.1 = f32[256,128]{1,0:T(8,128)} custom-call(f32[256,128]{1,0:T(8,128)} %bitcast.6, f32[256,128]{1,0:T(8,128)} %bitcast.7, f32[256,128]{1,0:T(8,128)} %bitcast.8, f32[256,128]{1,0:T(8,128)} %bitcast.9), custom_call_target="tpu_custom_call" | custom-call | tf_op jit(solution)/shard_map/vcycle/pallas_call | solution.py:1012
  54.0 1.6 %copy.6 = f32[16,16,128]{2,1,0:T(8,128)} copy(f32[16,16,128]{2,1,0:T(8,128)} %bitcast.5) | data formatting | bytes 262144

commit v4 on v3

--- a/solution.py
+++ b/solution.py
@@ -102,20 +102,27 @@
 dma("hw_ss", 26)
 dma("hw_rs", 26)
 vmem("q1", 8 * 16, 128)
-vmem("h1", 6, 8, 128)
-for key, rows, count in (("a0", 16, 3), ("b", 16, 6), ("c", 16, 6), ("h", 16, 6), ("a1", 8, 3), ("d", 8, 6), ("e", 8, 6)):
+for key, rows, count in (("a0", 16, 3), ("b", 16, 6), ("c", 16, 6), ("a1", 8, 3), ("d", 8, 6), ("e", 8, 6)):
     vmem(f"{key}_snd", count, rows, 128)
     vmem(f"{key}_rcv", count, rows, 128)
     dma(f"{key}_ss", count)
     dma(f"{key}_rs", count)
+vmem("t0", 256, 128)
+vmem("hh_snd", 6, 7, 16, 128)
+vmem("hh_rcv", 6, 7, 16, 128)
+dma("hh_ss", 6)
+dma("hh_rs", 6)
+vmem("side1", 6, 16, 128)
+vmem("wide1", 6, 4, 16, 128)
 vmem("t16", 3, 16, 128)
-vmem("zf_snd", 4, 3, 16, 128)
-vmem("zf_rcv", 7, 4, 3, 16, 128)
+vmem("zf_snd", 3, 16, 128)
+vmem("zf_rcv", 7, 3, 16, 128)
+vmem("xf_snd", 3, 6, 16, 128)
+vmem("xf_rcv", 3, 3, 6, 16, 128)
 vmem("zr_snd", 16, 128)
 vmem("zr_rcv", 7, 16, 128)
 vmem("xr_snd", 2, 16, 128)
 vmem("xr_rcv", 11, 2, 16, 128)
-vmem("m2", 6, 16, 128)
 for key, count in (("zf", 7), ("zr", 7), ("xr", 11), ("xf", 3), ("nf", 2)):
     dma(f"{key}_ss", count)
     dma(f"{key}_rs", count)
@@ -313,6 +320,7 @@
 
         def emit(i, v, total):
             r[block.own(i)] = d15[block.own(i)] * (total - RELAX * v)
+            s.t0[block.own(i)] = v * THIRD + total
 
         stencil(level, source, low, high, emit)
 
@@ -325,7 +333,7 @@
     flat_yr = [(x, y) for x in (1, -1, 0) for y in (1, -1)]
     flat_zr = [(x, y, z) for x in (1, -1, 0) for y in (1, -1, 0) for z in (1, -1)]
 
-    def send_around():
+    def pack_around():
         zeds = [jnp.zeros((8, 128), F32)] * 2
         group = lane8 // 3
         for a in range(5):
@@ -349,6 +357,7 @@
                 s.hw_low[t, i] = jnp.where(upper_half, even, turn(odd, 4, 0))
                 s.hw_high[t, i] = jnp.where(upper_half, turn(even, 4, 0), odd)
 
+    def send_around():
         def source(k):
             x, y, z = AROUND[k]
             if z != 0:
@@ -523,9 +532,9 @@
         s.t16[2, own] = total * 0.25
     s.t16[0] = pair_z(s.t16[0]) * 0.25
     s.t16[1] = pair_z(s.t16[1]) * 0.25
-    stage_z(3, s.zf_snd.at[0, 0])
+    stage_z(3, s.zf_snd.at[0])
     round_nf = copies(
-        SIDES, lambda k: s.zf_snd.at[0, 0], lambda k: s.zf_snd.at[0, k + 1], s.nf_ss, s.nf_rs
+        SIDES, lambda k: s.zf_snd.at[0], lambda k: s.zf_snd.at[k + 1], s.nf_ss, s.nf_rs
     )
     for ref in (s.va1, s.vb1):
         for k in (-1, 17):
@@ -572,10 +581,6 @@
     s.ext1[1, pl.ds(16 * 4 + 8, 8, stride=16)] = s.a1_rcv[1]
     coefficients1(4, 11)
     finish(round_b)
-    finish(round_nf)
-    round_xf = copies(
-        LINE, lambda k: s.zf_snd.at[0], lambda k: s.zf_snd.at[k + 1], s.xf_ss, s.xf_rs
-    )
     fill(B0, s.va0, s.b_rcv)
     smooth(0, s.va0, s.vb0, s.b_rcv[4], s.b_rcv[5])
     round_c = send_faces(B0, s.vb0, "c")
@@ -594,16 +599,31 @@
         s.va1[pl.ds(16 * (i + 5), 8)] = start
         s.va1[pl.ds(16 * (i + 5) + 8, 8)] = jnp.zeros((8, 128), F32)
     round_d = send_faces1(s.va1, "d")
-    finish(round_xf)
+    finish(round_nf)
     round_zf = copies(
         RING_Z, lambda k: s.zf_snd, lambda k: s.zf_rcv.at[k], s.zf_ss, s.zf_rs
     )
+    kept = (s.t0, s.cxl0, s.cxu0, s.cyl0, s.cyu0, s.czl0, s.czu0)
+    for a, ref in enumerate(kept):
+        s.hh_snd[0, a] = ref[B0.own(15)]
+        s.hh_snd[1, a] = ref[B0.own(0)]
+        s.hh_snd[2, a] = ref[pl.ds(15, 16, stride=16)]
+        s.hh_snd[3, a] = ref[pl.ds(0, 16, stride=16)]
+        s.hh_snd[4, a] = pack(lambda i: ref[B0.own(i)], 16, 16, 127)
+        s.hh_snd[5, a] = pack(lambda i: ref[B0.own(i)], 16, 16, 0)
     finish(round_d)
     fill1(s.va1, s.d_rcv)
     smooth1(4, 11, s.va1, s.vb1)
     for i in range(8):
         s.hw_own[4, i] = s.vb1[pl.ds(16 * (i + 5), 8)]
     round_e = send_faces1(s.vb1, "e")
+    finish(round_zf)
+    for side in range(3):
+        merge_z(3, s.zf_snd[side], lambda k: s.zf_rcv[k, side], s.xf_snd.at[side])
+    round_xf = copies(
+        LINE, lambda k: s.xf_snd, lambda k: s.xf_rcv.at[k], s.xf_ss, s.xf_rs
+    )
+    pack_around()
 
 
     def block2(p, x):
@@ -673,7 +693,6 @@
 
 
     mine = pl.ds(pl.multiple_of(16 * gy, 16), 16)
-    round_hw = send_around()
 
     def stencil2(ref, emit):
         for p in range(2):
@@ -698,16 +717,17 @@
         PLANE, lambda k: s.xr_snd, lambda k: s.xr_rcv.at[k], s.xr_ss, s.xr_rs
     )
 
-    finish(round_zf)
+    round_hw = send_around()
+    finish(round_xf)
     for line in range(4):
         first = 4 * ((gx - ((0, 0, 0), *LINE)[line][0]) & 3)
         for side in range(3):
+            part = s.xf_snd.at[side] if line == 0 else s.xf_rcv.at[line - 1, side]
             place = pl.ds((4, 0, 8)[side], 4)
-            merge_z(3, s.zf_snd[line, side], lambda k: s.zf_rcv[k, line, side], s.m2)
             for a in range(3):
                 for p in range(2):
                     for x in range(4):
-                        piece = s.m2[2 * a + p, pl.ds(4 * x, 4)]
+                        piece = part[2 * a + p, pl.ds(4 * x, 4)]
                         faces2[a][p, x + 2 + first, place] = piece
     for a, ref in enumerate((s.lx2, s.ly2, s.lz2)):
         for i in range(8):
@@ -778,6 +798,9 @@
         RING_Y, lambda k: s.f3.at[mine], lambda k: s.f3.at[mine], s.yr_ss, s.yr_rs
     )
     round_nv = send_sides((s.vb2,), "nv")
+    round_hh = copies(
+        FACES, lambda k: s.hh_snd.at[k], lambda k: s.hh_rcv.at[k], s.hh_ss, s.hh_rs
+    )
 
     finish(round_yf)
     zero8 = jnp.zeros((8, 128), F32)
@@ -976,13 +999,7 @@
                 s.vb1[pad1(i)] = s.vb1[pad1(i)] + more
     smooth1(2, 13, s.vb1, s.va1)
     smooth1(3, 12, s.va1, s.vb1)
-    s.h1[0] = s.vb1[pl.ds(16 * 4, 8)]
-    s.h1[1] = s.vb1[pl.ds(16 * 13, 8)]
-    s.h1[2] = s.vb1[pl.ds(16 * 5 + 15, 8, stride=16)]
-    s.h1[3] = s.vb1[pl.ds(16 * 5 + 8, 8, stride=16)]
     inner = lambda i: s.vb1[pl.ds(16 * (i + 5), 8)]
-    s.h1[4] = pack(inner, 8, 8, 127)
-    s.h1[5] = pack(inner, 8, 8, 64)
 
     def widen(value, ref, start):
         ref[pl.ds(start, 8, stride=2)] = value
@@ -993,18 +1010,59 @@
         more = widen(inner(i), s.w0, 16 * i)
         for x in (2 * i, 2 * i + 1):
             s.vb0[B0.at(x)] = s.vb0[B0.at(x)] + more
+
+    sides = [s.vb1[pl.ds(16 * 4, 16)], s.vb1[pl.ds(16 * 13, 16)]]
+    near = [inner(0), inner(7)]
+    for k, row, edge in ((2, 15, 0), (3, 8, 7)):
+        s.side1[k, pl.ds(8, 8)] = jnp.zeros((8, 128), F32)
+        s.side1[k, pl.ds(0, 8)] = s.vb1[pl.ds(16 * 5 + row, 8, stride=16)]
+        s.side1[k, pl.ds(8, 1)] = s.vb1[pl.ds(16 * 13 + row, 1)]
+        s.side1[k, pl.ds(15, 1)] = s.vb1[pl.ds(16 * 4 + row, 1)]
+        sides.append(s.side1[k])
+        near.append(s.vb1[pl.ds(16 * 5 + edge, 8, stride=16)])
+    for column, edge in ((127, 0), (64, 63)):
+        packed = jnp.zeros((16, 128), F32)
+        for k in range(3, 13):
+            place = (k - 4) & 127
+            packed = jnp.where(lane16 == place, turn(s.vb1[pad1(k)], place - column), packed)
+        sides.append(packed)
+        near.append(pack(inner, 8, 8, edge))
+
+    def tall(value, ref):
+        ref[pl.ds(0, 8, stride=2)] = value
+        ref[pl.ds(1, 8, stride=2)] = value
+        return ref[...]
+
+    first_row, first_lane = (row16 & 1) == 0, (lane16 & 1) == 0
+    layers = []
+    finish(round_hh)
     for k in range(6):
-        s.c_rcv[k] = s.c_rcv[k] + widen(s.h1[k], s.w0, 128 + 16 * k)
+        side = sides[k]
+        rows = tall(side[0:8], s.wide1.at[k, 0])
+        here = take(rows, half16)
+        inside = take(tall(near[k], s.wide1.at[k, 1]), half16)
+        before = take(tall(turn(side, 1, 0)[0:8], s.wide1.at[k, 2]), half16)
+        after = take(tall(turn(side, -1, 0)[0:8], s.wide1.at[k, 3]), half16)
+        row_low = jnp.where(first_row, before, here)
+        row_high = jnp.where(first_row, here, after)
+        lane_low = jnp.where(first_lane, take(turn(rows, 1), half16), here)
+        lane_high = jnp.where(first_lane, here, take(turn(rows, -1), half16))
+        axis = k // 2
+        of_rows, of_lanes = ((1, 2), (0, 2), (1, 0))[axis]
+        c = lambda d, upper: s.hh_rcv[k, 1 + 2 * d + upper]
+        upper = 1 - k % 2
+        total = s.hh_rcv[k, 0] + (THIRD + c(axis, 1 - upper)) * here + c(axis, upper) * inside
+        total = total + c(of_rows, 0) * row_low + c(of_rows, 1) * row_high
+        layers.append(total + (c(of_lanes, 0) * lane_low + c(of_lanes, 1) * lane_high))
+        s.c_rcv[k] = s.c_rcv[k] + here
     fill(B0, s.vb0, s.c_rcv)
     smooth(0, s.vb0, s.va0, s.c_rcv[4], s.c_rcv[5])
-    round_h = send_faces(B0, s.va0, "h")
-    finish(round_h)
-    fill(B0, s.va0, s.h_rcv)
+    fill(B0, s.va0, layers)
 
     def emit_out(i, v, total):
         out[B0.own(i)] = v * THIRD + total
 
-    stencil(0, s.va0, s.h_rcv[4], s.h_rcv[5], emit_out)
+    stencil(0, s.va0, layers[4], layers[5], emit_out)
 
 
 def shards(rhs, face_x, face_y, face_z):

time: 55.6 us -> 52.8 us (0.950)
  Pallas kernels: 54 us -> 51.2 us
    pallas_call x1, Pallas kernels: 54 us -> 51.2 us  [shards(): pl.pallas_call(cycle, out_shape=jax.ShapeDtypeStruct((256, 128), F32), in...]
where the time goes in v4:
time: 52.8 us; the launch traced here: 52.7 us
  Pallas kernels  51.2 us (97%)
  local copies, waits for them, and re-layouts  1.57 us (3%)
    pallas_call x1, Pallas kernels, shards(): pl.pallas_call(cycle, out_shape=jax.ShapeDtypeStruct((256, 128), F32), in...  51.2 us
    unnamed x1, local copies, waits for them, and re-layouts  1.57 us

profile of v4, /device:TPU:1, one launch (start us, length us, event | category | flops | bytes accessed | tf_op | source)
XLA Modules:
  0.0 52.7 jit_solution(8608610864656413481)
XLA Ops:
  0.0 51.2 %vcycle.1 = f32[256,128]{1,0:T(8,128)} custom-call(f32[256,128]{1,0:T(8,128)} %bitcast.6, f32[256,128]{1,0:T(8,128)} %bitcast.7, f32[256,128]{1,0:T(8,128)} %bitcast.8, f32[256,128]{1,0:T(8,128)} %bitcast.9), custom_call_target="tpu_custom_call" | custom-call | tf_op jit(solution)/shard_map/vcycle/pallas_call | solution.py:1070
  51.2 1.6 %copy.6 = f32[16,16,128]{2,1,0:T(8,128)} copy(f32[16,16,128]{2,1,0:T(8,128)} %bitcast.5) | data formatting | bytes 262144

commit v5 on v4

--- a/solution.py
+++ b/solution.py
@@ -21,6 +21,7 @@
 ]
 AROUND.sort(key=lambda d: -(abs(d[0]) + abs(d[1]) + abs(d[2])))
 LINE = [(2, 0, 0), (1, 0, 0), (3, 0, 0)]
+FRIENDS = [(0, 0, 4), (0, 0, 3), (0, 0, 5), (0, 0, 2), (0, 0, 6)] + FACES
 SIDES = [(0, 1, 0), (0, -1, 0)]
 PLANE = [(2, 1, 0), (2, -1, 0), (1, 1, 0), (1, -1, 0), (3, 1, 0), (3, -1, 0)]
 PLANE += [(2, 0, 0), (0, 1, 0), (0, -1, 0), (1, 0, 0), (3, 0, 0)]
@@ -179,7 +180,7 @@
         load.start()
 
     barrier = pltpu.get_barrier_semaphore()
-    for offset in FACES:
+    for offset in FRIENDS:
         pl.semaphore_signal(barrier, inc=1, device_id=peer(offset), device_id_type=MESH)
 
     def copies(offsets, sources, targets, ss, rs):
@@ -198,11 +199,17 @@
             one.start()
         return made
 
+    sent = []
+
     def finish(made):
         for one in made:
             one.wait_recv()
-        for one in made:
+        sent.extend(made)
+
+    def drain():
+        for one in sent:
             one.wait_send()
+        sent.clear()
 
     def flag(condition):
         return jnp.where(condition, 1.0, 0.0).astype(F32)
@@ -248,7 +255,7 @@
         snd[1] = ly[pl.ds(0, block.X, stride=block.Y)]
         snd[2] = pack(lambda i: lz[block.own(i)], 16, 16, 0)
         rcv = getattr(s, key + "_rcv")
-        pl.semaphore_wait(barrier, len(FACES))
+        pl.semaphore_wait(barrier, len(FRIENDS))
         return copies(
             DOWN,
             lambda k: snd.at[k],
@@ -567,6 +574,10 @@
         s.g0[own] = start
         s.va0[B0.at(i)] = start
     round_b = send_faces(B0, s.va0, "b")
+    finish(round_nf)
+    round_zf = copies(
+        RING_Z, lambda k: s.zf_snd, lambda k: s.zf_rcv.at[k], s.zf_ss, s.zf_rs
+    )
     finish(round_a1)
     for i in range(8):
         own, here = pl.ds(8 * i, 8), pl.ds(16 * (i + 4), 8)
@@ -584,6 +595,12 @@
     fill(B0, s.va0, s.b_rcv)
     smooth(0, s.va0, s.vb0, s.b_rcv[4], s.b_rcv[5])
     round_c = send_faces(B0, s.vb0, "c")
+    finish(round_zf)
+    for side in range(3):
+        merge_z(3, s.zf_snd[side], lambda k: s.zf_rcv[k, side], s.xf_snd.at[side])
+    round_xf = copies(
+        LINE, lambda k: s.xf_snd, lambda k: s.xf_rcv.at[k], s.xf_ss, s.xf_rs
+    )
     finish(round_c)
     fill(B0, s.vb0, s.c_rcv)
     residual(0, s.vb0, s.c_rcv[4], s.c_rcv[5])
@@ -599,10 +616,6 @@
         s.va1[pl.ds(16 * (i + 5), 8)] = start
         s.va1[pl.ds(16 * (i + 5) + 8, 8)] = jnp.zeros((8, 128), F32)
     round_d = send_faces1(s.va1, "d")
-    finish(round_nf)
-    round_zf = copies(
-        RING_Z, lambda k: s.zf_snd, lambda k: s.zf_rcv.at[k], s.zf_ss, s.zf_rs
-    )
     kept = (s.t0, s.cxl0, s.cxu0, s.cyl0, s.cyu0, s.czl0, s.czu0)
     for a, ref in enumerate(kept):
         s.hh_snd[0, a] = ref[B0.own(15)]
@@ -617,12 +630,6 @@
     for i in range(8):
         s.hw_own[4, i] = s.vb1[pl.ds(16 * (i + 5), 8)]
     round_e = send_faces1(s.vb1, "e")
-    finish(round_zf)
-    for side in range(3):
-        merge_z(3, s.zf_snd[side], lambda k: s.zf_rcv[k, side], s.xf_snd.at[side])
-    round_xf = copies(
-        LINE, lambda k: s.xf_snd, lambda k: s.xf_rcv.at[k], s.xf_ss, s.xf_rs
-    )
     pack_around()
 
 
@@ -674,50 +681,8 @@
     global_y = row16 + 4 * gy - 4
     not_low, not_top = global_y != 0, global_y != 4 * GY - 1
 
-    finish(round_e)
-    fill1(s.vb1, s.e_rcv)
-
-    def emit_r1(k, v, total):
-        r = s.d151[ext1(k)] * (total - RELAX * v)
-        s.r1[pl.ds(8 * (k - 4), 8)] = r[0:8]
-
-    stencil1(4, 11, s.vb1, emit_r1)
-    for i in range(4):
-        here = lambda shift: s.r1[pl.ds(16 * i + shift, 4, stride=2)]
-        s.t16[0, pl.ds(4 * i, 4)] = (here(0) + here(1)) + (here(8) + here(9))
-    s.t16[0] = pair_z(s.t16[0]) * 0.125
-    stage_z(1, s.zr_snd)
-    round_zr = copies(
-        RING_Z, lambda k: s.zr_snd, lambda k: s.zr_rcv.at[k], s.zr_ss, s.zr_rs
-    )
-
-
     mine = pl.ds(pl.multiple_of(16 * gy, 16), 16)
 
-    def stencil2(ref, emit):
-        for p in range(2):
-            for x in range(16):
-                j, other = block2(p, x), block2(1 - p, x)
-                v, w = ref[j], ref[other]
-                t_x = s.cxl2[j] * ref[block2(p, x - 1)] + s.cxu2[j] * ref[block2(p, x + 1)]
-                t_y = s.cyl2[j] * turn(v, 1, 0) + s.cyu2[j] * turn(v, -1, 0)
-                down, up = (turn(w, 1), w) if p == 0 else (w, turn(w, -1))
-                t_z = s.czl2[j] * down + s.czu2[j] * up
-                emit(j, v, s.g2[j] + (t_x + t_y + t_z))
-
-    def smooth2(source, target):
-        def emit(j, v, total):
-            target[j] = v * THIRD + total
-
-        stencil2(source, emit)
-
-    finish(round_zr)
-    merge_z(1, s.zr_snd[...], lambda k: s.zr_rcv[k], s.xr_snd)
-    round_xr = copies(
-        PLANE, lambda k: s.xr_snd, lambda k: s.xr_rcv.at[k], s.xr_ss, s.xr_rs
-    )
-
-    round_hw = send_around()
     finish(round_xf)
     for line in range(4):
         first = 4 * ((gx - ((0, 0, 0), *LINE)[line][0]) & 3)
@@ -751,6 +716,42 @@
         s.yf_ss,
         s.yf_rs,
     )
+    finish(round_e)
+    fill1(s.vb1, s.e_rcv)
+
+    def emit_r1(k, v, total):
+        r = s.d151[ext1(k)] * (total - RELAX * v)
+        s.r1[pl.ds(8 * (k - 4), 8)] = r[0:8]
+
+    stencil1(4, 11, s.vb1, emit_r1)
+    for i in range(4):
+        here = lambda shift: s.r1[pl.ds(16 * i + shift, 4, stride=2)]
+        s.t16[0, pl.ds(4 * i, 4)] = (here(0) + here(1)) + (here(8) + here(9))
+    s.t16[0] = pair_z(s.t16[0]) * 0.125
+    stage_z(1, s.zr_snd)
+    round_zr = copies(
+        RING_Z, lambda k: s.zr_snd, lambda k: s.zr_rcv.at[k], s.zr_ss, s.zr_rs
+    )
+
+
+    def stencil2(ref, emit):
+        for p in range(2):
+            for x in range(16):
+                j, other = block2(p, x), block2(1 - p, x)
+                v, w = ref[j], ref[other]
+                t_x = s.cxl2[j] * ref[block2(p, x - 1)] + s.cxu2[j] * ref[block2(p, x + 1)]
+                t_y = s.cyl2[j] * turn(v, 1, 0) + s.cyu2[j] * turn(v, -1, 0)
+                down, up = (turn(w, 1), w) if p == 0 else (w, turn(w, -1))
+                t_z = s.czl2[j] * down + s.czu2[j] * up
+                emit(j, v, s.g2[j] + (t_x + t_y + t_z))
+
+    def smooth2(source, target):
+        def emit(j, v, total):
+            target[j] = v * THIRD + total
+
+        stencil2(source, emit)
+
+    round_hw = send_around()
     for p in range(2):
         for x in range(16):
             j = block2(p, x)
@@ -772,34 +773,10 @@
             s.czl2[j] = scale * a_zl if p == 1 else jnp.where(lane16 == 0, 0.0, scale * a_zl)
             s.czu2[j] = scale * a_zu
 
-    finish(round_xr)
-    spread(1, PLANE, s.xr_snd, s.xr_rcv, (s.f2,))
-    for p in range(2):
-        for x in range(16):
-            j = block2(p, x)
-            start = s.kw2[j] * s.f2[j]
-            s.g2[j] = start
-            s.va2[j] = start
-    smooth2(s.va2, s.vb2)
-
-    def emit_r2(j, v, total):
-        s.f2[j] = s.d152[j] * (total - RELAX * v)
-
-    stencil2(s.vb2, emit_r2)
-    for i in range(8):
-        total = (s.f2[block2(0, 2 * i)] + s.f2[block2(1, 2 * i)]) + (
-            s.f2[block2(0, 2 * i + 1)] + s.f2[block2(1, 2 * i + 1)]
-        )
-        s.s2[pl.ds(16 * i, 16)] = total
-    for j in range(2):
-        total = s.s2[pl.ds(4 + 2 * j, 8, stride=16)] + s.s2[pl.ds(5 + 2 * j, 8, stride=16)]
-        s.f3[pl.ds(pl.multiple_of(16 * gy + 8 * j, 8), 8)] = total * 0.125
-    round_yr = copies(
-        RING_Y, lambda k: s.f3.at[mine], lambda k: s.f3.at[mine], s.yr_ss, s.yr_rs
-    )
-    round_nv = send_sides((s.vb2,), "nv")
-    round_hh = copies(
-        FACES, lambda k: s.hh_snd.at[k], lambda k: s.hh_rcv.at[k], s.hh_ss, s.hh_rs
+    finish(round_zr)
+    merge_z(1, s.zr_snd[...], lambda k: s.zr_rcv[k], s.xr_snd)
+    round_xr = copies(
+        PLANE, lambda k: s.xr_snd, lambda k: s.xr_rcv.at[k], s.xr_ss, s.xr_rs
     )
 
     finish(round_yf)
@@ -886,6 +863,37 @@
     s.czl5[...] = jnp.where(lane8 < 4, 0.0, scale * a_zl)
     s.czu5[...] = scale * a_zu
 
+    finish(round_xr)
+    spread(1, PLANE, s.xr_snd, s.xr_rcv, (s.f2,))
+    for p in range(2):
+        for x in range(16):
+            j = block2(p, x)
+            start = s.kw2[j] * s.f2[j]
+            s.g2[j] = start
+            s.va2[j] = start
+    smooth2(s.va2, s.vb2)
+
+    def emit_r2(j, v, total):
+        s.f2[j] = s.d152[j] * (total - RELAX * v)
+
+    stencil2(s.vb2, emit_r2)
+    for i in range(8):
+        total = (s.f2[block2(0, 2 * i)] + s.f2[block2(1, 2 * i)]) + (
+            s.f2[block2(0, 2 * i + 1)] + s.f2[block2(1, 2 * i + 1)]
+        )
+        s.s2[pl.ds(16 * i, 16)] = total
+    for j in range(2):
+        total = s.s2[pl.ds(4 + 2 * j, 8, stride=16)] + s.s2[pl.ds(5 + 2 * j, 8, stride=16)]
+        s.f3[pl.ds(pl.multiple_of(16 * gy + 8 * j, 8), 8)] = total * 0.125
+    round_yr = copies(
+        RING_Y, lambda k: s.f3.at[mine], lambda k: s.f3.at[mine], s.yr_ss, s.yr_rs
+    )
+    round_nv = send_sides((s.vb2,), "nv")
+    round_hh = copies(
+        FACES, lambda k: s.hh_snd.at[k], lambda k: s.hh_rcv.at[k], s.hh_ss, s.hh_rs
+    )
+
+    drain()
     finish(round_hw)
     for k in range(1, 15):
         for a in range(4):
@@ -1036,6 +1044,7 @@
     first_row, first_lane = (row16 & 1) == 0, (lane16 & 1) == 0
     layers = []
     finish(round_hh)
+    drain()
     for k in range(6):
         side = sides[k]
         rows = tall(side[0:8], s.wide1.at[k, 0])

time: 52.8 us -> 50.8 us (0.962)
  Pallas kernels: 51.2 us -> 49.1 us
    pallas_call x1, Pallas kernels: 51.2 us -> 49.1 us  [shards(): pl.pallas_call(cycle, out_shape=jax.ShapeDtypeStruct((256, 128), F32), in...]
where the time goes in v5:
time: 50.8 us; the launch traced here: 50.7 us
  Pallas kernels  49.1 us (97%)
  local copies, waits for them, and re-layouts  1.57 us (3%)
    pallas_call x1, Pallas kernels, shards(): pl.pallas_call(cycle, out_shape=jax.ShapeDtypeStruct((256, 128), F32), in...  49.1 us
    unnamed x1, local copies, waits for them, and re-layouts  1.57 us

profile of v5, /device:TPU:1, one launch (start us, length us, event | category | flops | bytes accessed | tf_op | source)
XLA Modules:
  0.0 50.7 jit_solution(12351425661287587654)
XLA Ops:
  0.0 49.1 %vcycle.1 = f32[256,128]{1,0:T(8,128)} custom-call(f32[256,128]{1,0:T(8,128)} %bitcast.6, f32[256,128]{1,0:T(8,128)} %bitcast.7, f32[256,128]{1,0:T(8,128)} %bitcast.8, f32[256,128]{1,0:T(8,128)} %bitcast.9), custom_call_target="tpu_custom_call" | custom-call | tf_op jit(solution)/shard_map/vcycle/pallas_call | solution.py:1079
  49.1 1.6 %copy.6 = f32[16,16,128]{2,1,0:T(8,128)} copy(f32[16,16,128]{2,1,0:T(8,128)} %bitcast.5) | data formatting | bytes 262144

commit v6 on v5

--- a/solution.py
+++ b/solution.py
@@ -116,10 +116,12 @@
 vmem("side1", 6, 16, 128)
 vmem("wide1", 6, 4, 16, 128)
 vmem("t16", 3, 16, 128)
-vmem("zf_snd", 3, 16, 128)
-vmem("zf_rcv", 7, 3, 16, 128)
-vmem("xf_snd", 3, 6, 16, 128)
-vmem("xf_rcv", 3, 3, 6, 16, 128)
+vmem("zf_snd", 16, 128)
+vmem("zf_rcv", 7, 16, 128)
+vmem("xf_snd", 6, 16, 128)
+vmem("xf_rcv", 3, 6, 16, 128)
+vmem("nf_snd", 3, 2, 8, 8, 128)
+vmem("nf_rcv", 2, 3, 2, 8, 8, 128)
 vmem("zr_snd", 16, 128)
 vmem("zr_rcv", 7, 16, 128)
 vmem("xr_snd", 2, 16, 128)
@@ -183,7 +185,7 @@
     for offset in FRIENDS:
         pl.semaphore_signal(barrier, inc=1, device_id=peer(offset), device_id_type=MESH)
 
-    def copies(offsets, sources, targets, ss, rs):
+    def copies(offsets, sources, targets, ss, rs, first=0):
         made = [
             pltpu.make_async_remote_copy(
                 src_ref=sources(k),
@@ -193,7 +195,7 @@
                 device_id=peer(offset),
                 device_id_type=MESH,
             )
-            for k, offset in enumerate(offsets)
+            for k, offset in enumerate(offsets, first)
         ]
         for one in made:
             one.start()
@@ -226,21 +228,17 @@
         return packed
 
     def send_faces(block, ref, key):
-        snd = getattr(s, key + "_snd")
+        snd, rcv = getattr(s, key + "_snd"), getattr(s, key + "_rcv")
         snd[0] = ref[block.at(block.X - 1)]
         snd[1] = ref[block.at(0)]
         snd[2] = ref[block.row_of_each(block.Y - 1)]
         snd[3] = ref[block.row_of_each(0)]
+        sems = getattr(s, key + "_ss"), getattr(s, key + "_rs")
+        ends = (lambda k: snd.at[k], lambda k: rcv.at[k], *sems)
+        made = copies(FACES[:4], *ends)
         snd[4] = pack(lambda i: ref[block.at(i)], 16, 16, 127)
         snd[5] = pack(lambda i: ref[block.at(i)], 16, 16, 0)
-        rcv = getattr(s, key + "_rcv")
-        return copies(
-            FACES,
-            lambda k: snd.at[k],
-            lambda k: rcv.at[k],
-            getattr(s, key + "_ss"),
-            getattr(s, key + "_rs"),
-        )
+        return made + copies(FACES[4:], *ends, first=4)
 
     def fill(block, ref, halo):
         ref[block.at(-1)] = halo[0]
@@ -452,15 +450,12 @@
         snd[1] = inner(0)
         snd[2] = ref[pl.ds(16 * 5 + 7, 8, stride=16)]
         snd[3] = ref[pl.ds(16 * 5, 8, stride=16)]
+        sems = getattr(s, key + "_ss"), getattr(s, key + "_rs")
+        ends = (lambda k: snd.at[k], lambda k: rcv.at[k], *sems)
+        made = copies(FACES[:4], *ends)
         snd[4] = pack(inner, 8, 8, 63)
         snd[5] = pack(inner, 8, 8, 0)
-        return copies(
-            FACES,
-            lambda k: snd.at[k],
-            lambda k: rcv.at[k],
-            getattr(s, key + "_ss"),
-            getattr(s, key + "_rs"),
-        )
+        return made + copies(FACES[4:], *ends, first=4)
 
     def fill1(ref, halo):
         low, high = halo[4], halo[5]
@@ -539,17 +534,11 @@
         s.t16[2, own] = total * 0.25
     s.t16[0] = pair_z(s.t16[0]) * 0.25
     s.t16[1] = pair_z(s.t16[1]) * 0.25
-    stage_z(3, s.zf_snd.at[0])
-    round_nf = copies(
-        SIDES, lambda k: s.zf_snd.at[0], lambda k: s.zf_snd.at[k + 1], s.nf_ss, s.nf_rs
+    stage_z(3, s.zf_snd)
+    round_zf = copies(
+        RING_Z, lambda k: s.zf_snd, lambda k: s.zf_rcv.at[k], s.zf_ss, s.zf_rs
     )
-    for ref in (s.va1, s.vb1):
-        for k in (-1, 17):
-            ref[pad1(k)] = jnp.zeros((16, 128), F32)
     for p in range(2):
-        for x in range(16):
-            for ref in (s.lx2, s.ly2, s.lz2):
-                ref[p, x + 2, pl.ds(8, 8)] = jnp.ones((8, 128), F32)
         for x in (0, 1, 18, 19):
             for ref in (s.va2, s.vb2):
                 ref[p, x] = jnp.zeros((16, 128), F32)
@@ -574,10 +563,6 @@
         s.g0[own] = start
         s.va0[B0.at(i)] = start
     round_b = send_faces(B0, s.va0, "b")
-    finish(round_nf)
-    round_zf = copies(
-        RING_Z, lambda k: s.zf_snd, lambda k: s.zf_rcv.at[k], s.zf_ss, s.zf_rs
-    )
     finish(round_a1)
     for i in range(8):
         own, here = pl.ds(8 * i, 8), pl.ds(16 * (i + 4), 8)
@@ -591,13 +576,12 @@
     s.ext1[0, pl.ds(16 * 12, 8)] = s.a1_rcv[0]
     s.ext1[1, pl.ds(16 * 4 + 8, 8, stride=16)] = s.a1_rcv[1]
     coefficients1(4, 11)
+    finish(round_zf)
+    merge_z(3, s.zf_snd[...], lambda k: s.zf_rcv[k], s.xf_snd)
     finish(round_b)
     fill(B0, s.va0, s.b_rcv)
     smooth(0, s.va0, s.vb0, s.b_rcv[4], s.b_rcv[5])
     round_c = send_faces(B0, s.vb0, "c")
-    finish(round_zf)
-    for side in range(3):
-        merge_z(3, s.zf_snd[side], lambda k: s.zf_rcv[k, side], s.xf_snd.at[side])
     round_xf = copies(
         LINE, lambda k: s.xf_snd, lambda k: s.xf_rcv.at[k], s.xf_ss, s.xf_rs
     )
@@ -615,23 +599,6 @@
         s.g1[pl.ds(16 * (i + 4) + 8, 8)] = jnp.zeros((8, 128), F32)
         s.va1[pl.ds(16 * (i + 5), 8)] = start
         s.va1[pl.ds(16 * (i + 5) + 8, 8)] = jnp.zeros((8, 128), F32)
-    round_d = send_faces1(s.va1, "d")
-    kept = (s.t0, s.cxl0, s.cxu0, s.cyl0, s.cyu0, s.czl0, s.czu0)
-    for a, ref in enumerate(kept):
-        s.hh_snd[0, a] = ref[B0.own(15)]
-        s.hh_snd[1, a] = ref[B0.own(0)]
-        s.hh_snd[2, a] = ref[pl.ds(15, 16, stride=16)]
-        s.hh_snd[3, a] = ref[pl.ds(0, 16, stride=16)]
-        s.hh_snd[4, a] = pack(lambda i: ref[B0.own(i)], 16, 16, 127)
-        s.hh_snd[5, a] = pack(lambda i: ref[B0.own(i)], 16, 16, 0)
-    finish(round_d)
-    fill1(s.va1, s.d_rcv)
-    smooth1(4, 11, s.va1, s.vb1)
-    for i in range(8):
-        s.hw_own[4, i] = s.vb1[pl.ds(16 * (i + 5), 8)]
-    round_e = send_faces1(s.vb1, "e")
-    pack_around()
-
 
     def block2(p, x):
         return (p, x + 2)
@@ -681,19 +648,12 @@
     global_y = row16 + 4 * gy - 4
     not_low, not_top = global_y != 0, global_y != 4 * GY - 1
 
+    round_d = send_faces1(s.va1, "d")
     mine = pl.ds(pl.multiple_of(16 * gy, 16), 16)
 
     finish(round_xf)
-    for line in range(4):
-        first = 4 * ((gx - ((0, 0, 0), *LINE)[line][0]) & 3)
-        for side in range(3):
-            part = s.xf_snd.at[side] if line == 0 else s.xf_rcv.at[line - 1, side]
-            place = pl.ds((4, 0, 8)[side], 4)
-            for a in range(3):
-                for p in range(2):
-                    for x in range(4):
-                        piece = part[2 * a + p, pl.ds(4 * x, 4)]
-                        faces2[a][p, x + 2 + first, place] = piece
+    spread(3, LINE, s.xf_snd, s.xf_rcv, faces2)
+    round_nf = send_sides(faces2, "nf")
     for a, ref in enumerate((s.lx2, s.ly2, s.lz2)):
         for i in range(8):
             total = ref[block2(0, 2 * i)]
@@ -716,6 +676,22 @@
         s.yf_ss,
         s.yf_rs,
     )
+    finish(round_d)
+    fill1(s.va1, s.d_rcv)
+    smooth1(4, 11, s.va1, s.vb1)
+    for i in range(8):
+        s.hw_own[4, i] = s.vb1[pl.ds(16 * (i + 5), 8)]
+    round_e = send_faces1(s.vb1, "e")
+    kept = (s.t0, s.cxl0, s.cxu0, s.cyl0, s.cyu0, s.czl0, s.czu0)
+    for a, ref in enumerate(kept):
+        s.hh_snd[0, a] = ref[B0.own(15)]
+        s.hh_snd[1, a] = ref[B0.own(0)]
+        s.hh_snd[2, a] = ref[pl.ds(15, 16, stride=16)]
+        s.hh_snd[3, a] = ref[pl.ds(0, 16, stride=16)]
+        s.hh_snd[4, a] = pack(lambda i: ref[B0.own(i)], 16, 16, 127)
+        s.hh_snd[5, a] = pack(lambda i: ref[B0.own(i)], 16, 16, 0)
+    pack_around()
+
     finish(round_e)
     fill1(s.vb1, s.e_rcv)
 
@@ -752,6 +728,8 @@
         stencil2(source, emit)
 
     round_hw = send_around()
+    finish(round_nf)
+    take_sides(faces2, "nf", 1.0)
     for p in range(2):
         for x in range(16):
             j = block2(p, x)

time: 50.8 us -> 52.6 us (1.035)
  Pallas kernels: 49.1 us -> 50.9 us
    pallas_call x1, Pallas kernels: 49.1 us -> 50.9 us  [shards(): pl.pallas_call(cycle, out_shape=jax.ShapeDtypeStruct((256, 128), F32), in...]
where the time goes in v6:
time: 52.6 us; the launch traced here: 52.5 us
  Pallas kernels  50.9 us (97%)
  local copies, waits for them, and re-layouts  1.57 us (3%)
    pallas_call x1, Pallas kernels, shards(): pl.pallas_call(cycle, out_shape=jax.ShapeDtypeStruct((256, 128), F32), in...  50.9 us
    unnamed x1, local copies, waits for them, and re-layouts  1.57 us

profile of v6, /device:TPU:1, one launch (start us, length us, event | category | flops | bytes accessed | tf_op | source)
XLA Modules:
  0.0 52.5 jit_solution(12780504410846125872)
XLA Ops:
  0.0 50.9 %vcycle.1 = f32[256,128]{1,0:T(8,128)} custom-call(f32[256,128]{1,0:T(8,128)} %bitcast.6, f32[256,128]{1,0:T(8,128)} %bitcast.7, f32[256,128]{1,0:T(8,128)} %bitcast.8, f32[256,128]{1,0:T(8,128)} %bitcast.9), custom_call_target="tpu_custom_call" | custom-call | tf_op jit(solution)/shard_map/vcycle/pallas_call | solution.py:1057
  50.9 1.6 %copy.6 = f32[16,16,128]{2,1,0:T(8,128)} copy(f32[16,16,128]{2,1,0:T(8,128)} %bitcast.5) | data formatting | bytes 262144

commit v7 on v6

--- a/solution.py
+++ b/solution.py
@@ -122,6 +122,13 @@
 vmem("xf_rcv", 3, 6, 16, 128)
 vmem("nf_snd", 3, 2, 8, 8, 128)
 vmem("nf_rcv", 2, 3, 2, 8, 8, 128)
+for key in ("nf_half", "nf_mate"):
+    vmem(key, 2, 3, 2, 4, 8, 128)
+for key in ("face_half", "face_mate"):
+    vmem(key, 3, 8, 8, 128)
+for key in ("nm", "ym"):
+    dma(f"{key}_ss", 1)
+    dma(f"{key}_rs", 1)
 vmem("zr_snd", 16, 128)
 vmem("zr_rcv", 7, 16, 128)
 vmem("xr_snd", 2, 16, 128)
@@ -200,6 +207,21 @@
         for one in made:
             one.start()
         return made
+
+    core = gz & 1
+    mate = (gx, gy, gz + 1 - 2 * core)
+
+    def to_mate(source, target, key):
+        one = pltpu.make_async_remote_copy(
+            src_ref=source,
+            dst_ref=target,
+            send_sem=getattr(s, key + "_ss").at[0],
+            recv_sem=getattr(s, key + "_rs").at[0],
+            device_id=mate,
+            device_id_type=MESH,
+        )
+        one.start()
+        return [one]
 
     sent = []
 
@@ -616,21 +638,13 @@
                         piece = part(2 * a + p)[pl.ds(4 * x, 4)]
                         targets[a][p, x + 2 + first, place] = piece
 
-    def send_sides(refs, key):
-        snd, rcv = getattr(s, key + "_snd"), getattr(s, key + "_rcv")
+    def pack_sides(refs, snd):
         for a, ref in enumerate(refs):
             for p in range(2):
                 for i in range(8):
                     even = ref[p, 2 * i + 2, pl.ds(0, 8)]
                     odd = ref[p, 2 * i + 3, pl.ds(0, 8)]
                     snd[a, p, i] = jnp.where(upper_half, turn(even, 4, 0), odd)
-        return copies(
-            SIDES,
-            lambda k: snd,
-            lambda k: rcv.at[k],
-            getattr(s, key + "_ss"),
-            getattr(s, key + "_rs"),
-        )
 
     def take_sides(refs, key, rest):
         rcv = getattr(s, key + "_rcv")
@@ -653,7 +667,14 @@
 
     finish(round_xf)
     spread(3, LINE, s.xf_snd, s.xf_rcv, faces2)
-    round_nf = send_sides(faces2, "nf")
+    pack_sides(faces2, s.nf_snd)
+    round_nf = copies(
+        SIDES,
+        lambda k: s.nf_snd.at[:, :, pl.ds(4 * core, 4)],
+        lambda k: s.nf_half.at[k],
+        s.nf_ss,
+        s.nf_rs,
+    )
     for a, ref in enumerate((s.lx2, s.ly2, s.lz2)):
         for i in range(8):
             total = ref[block2(0, 2 * i)]
@@ -664,15 +685,17 @@
             if a == 1:
                 total = total + ref[block2(1, 2 * i + 1)]
             s.s2[pl.ds(16 * i, 16)] = total
+        halves = []
         for j in range(2):
             total = s.s2[pl.ds(4 + 2 * j, 8, stride=16)]
             if a != 1:
                 total = total + s.s2[pl.ds(5 + 2 * j, 8, stride=16)]
-            s.face3[a, pl.ds(pl.multiple_of(16 * gy + 8 * j, 8), 8)] = total * 0.25
+            halves.append(total * 0.25)
+        s.face_half[a, gy] = jnp.where(core == 0, halves[0], halves[1])
     round_yf = copies(
         RING_Y,
-        lambda k: s.face3.at[:, mine],
-        lambda k: s.face3.at[:, mine],
+        lambda k: s.face_half.at[:, gy],
+        lambda k: s.face_half.at[:, gy],
         s.yf_ss,
         s.yf_rs,
     )
@@ -691,6 +714,8 @@
         s.hh_snd[4, a] = pack(lambda i: ref[B0.own(i)], 16, 16, 127)
         s.hh_snd[5, a] = pack(lambda i: ref[B0.own(i)], 16, 16, 0)
     pack_around()
+    finish(round_nf)
+    round_nm = to_mate(s.nf_half, s.nf_mate, "nm")
 
     finish(round_e)
     fill1(s.vb1, s.e_rcv)
@@ -728,7 +753,15 @@
         stencil2(source, emit)
 
     round_hw = send_around()
-    finish(round_nf)
+    finish(round_yf)
+    round_ym = to_mate(s.face_half, s.face_mate, "ym")
+    finish(round_nm)
+    for k in range(2):
+        for a in range(3):
+            for p in range(2):
+                for i in range(4):
+                    s.nf_rcv[k, a, p, 4 * core + i] = s.nf_half[k, a, p, i]
+                    s.nf_rcv[k, a, p, 4 - 4 * core + i] = s.nf_mate[k, a, p, i]
     take_sides(faces2, "nf", 1.0)
     for p in range(2):
         for x in range(16):
@@ -757,7 +790,13 @@
         PLANE, lambda k: s.xr_snd, lambda k: s.xr_rcv.at[k], s.xr_ss, s.xr_rs
     )
 
-    finish(round_yf)
+    finish(round_ym)
+    for a in range(3):
+        for y in range(8):
+            first = pl.ds(pl.multiple_of(16 * y + 8 * core, 8), 8)
+            second = pl.ds(pl.multiple_of(16 * y + 8 - 8 * core, 8), 8)
+            s.face3[a, first] = s.face_half[a, y]
+            s.face3[a, second] = s.face_mate[a, y]
     zero8 = jnp.zeros((8, 128), F32)
     for y in range(16):
         own = pl.ds(8 * y, 8)
@@ -866,7 +905,10 @@
     round_yr = copies(
         RING_Y, lambda k: s.f3.at[mine], lambda k: s.f3.at[mine], s.yr_ss, s.yr_rs
     )
-    round_nv = send_sides((s.vb2,), "nv")
+    pack_sides((s.vb2,), s.nv_snd)
+    round_nv = copies(
+        SIDES, lambda k: s.nv_snd, lambda k: s.nv_rcv.at[k], s.nv_ss, s.nv_rs
+    )
     round_hh = copies(
         FACES, lambda k: s.hh_snd.at[k], lambda k: s.hh_rcv.at[k], s.hh_ss, s.hh_rs
     )

time: 52.6 us -> 48.9 us (0.930)
  Pallas kernels: 50.9 us -> 47.2 us
    pallas_call x1, Pallas kernels: 50.9 us -> 47.2 us  [shards(): pl.pallas_call(cycle, out_shape=jax.ShapeDtypeStruct((256, 128), F32), in...]
where the time goes in v7:
time: 48.9 us; the launch traced here: 48.8 us
  Pallas kernels  47.2 us (97%)
  local copies, waits for them, and re-layouts  1.57 us (3%)
    pallas_call x1, Pallas kernels, shards(): pl.pallas_call(cycle, out_shape=jax.ShapeDtypeStruct((256, 128), F32), in...  47.2 us
    unnamed x1, local copies, waits for them, and re-layouts  1.57 us

profile of v7, /device:TPU:1, one launch (start us, length us, event | category | flops | bytes accessed | tf_op | source)
XLA Modules:
  0.0 48.8 jit_solution(1134141288612923008)
XLA Ops:
  0.0 47.2 %vcycle.1 = f32[256,128]{1,0:T(8,128)} custom-call(f32[256,128]{1,0:T(8,128)} %bitcast.6, f32[256,128]{1,0:T(8,128)} %bitcast.7, f32[256,128]{1,0:T(8,128)} %bitcast.8, f32[256,128]{1,0:T(8,128)} %bitcast.9), custom_call_target="tpu_custom_call" | custom-call | tf_op jit(solution)/shard_map/vcycle/pallas_call | solution.py:1099
  47.2 1.6 %copy.6 = f32[16,16,128]{2,1,0:T(8,128)} copy(f32[16,16,128]{2,1,0:T(8,128)} %bitcast.5) | data formatting | bytes 262144
